TPU v7x, 128 devices: a whole 4x4x4 slice. The times are simulated.
128 devices in a mesh: pos: 16 (over x, z), tile: 8 (over y, core).
Axes of the slice: x: 4, y: 4, z: 4, core: 2. Of those that a mesh axis runs over, the one named last changes fastest.
Arguments:
- object_field: float32 [2, 2048, 8192], P(None, 'tile', 'pos'), may hold values from -6 to 6
- probe_field: float32 [2, 256, 256], replicated, may hold values from -6 to 6
- measured: float32 [2048, 256, 256], P(('pos', 'tile')), may hold values from 0.5 to 2.5
- offsets: int32 [2048, 2], P(('pos', 'tile')), may hold values from -128 to 8063, as said below
Outputs:
- object_grad: float32 [2, 2048, 8192], P(None, 'tile', 'pos')
- probe_grad: float32 [2, 256, 256], replicated
Inputs may be any that keep to these rules, and one draw needn't show every extreme that they name: `offsets`: position n belongs to device slab n // 16 = p * 8 + t; its patch centre (r + 128, c + 128) lies in tile rows t * 256 to t * 256 + 255 and tile columns p * 512 to p * 512 + 511.
All inputs are finite; a program needn't handle non-finite values.
Results may differ from a plain program's by a relative error of at most 0.0003.
Values sent between devices are 32-bit elements; how exact they have to be, the bound alone decides.
A program may use at most 128 MiB of HBM per device.

v0:
```python
import math

import jax
import jax.numpy as jnp
from jax import lax
from jax.sharding import PartitionSpec as P


def extended_2(block, sides, width):
    for axis, dim in sides:
        count = lax.axis_size(axis)
        forward = [(i, i + 1) for i in range(count - 1)]
        backward = [(target, source) for source, target in forward]
        low = lax.ppermute(
            lax.slice_in_dim(block, block.shape[dim] - width, None, axis=dim), axis, forward
        )
        high = lax.ppermute(lax.slice_in_dim(block, 0, width, axis=dim), axis, backward)
        block = jnp.concatenate([low, block, high], axis=dim)
    return block


def passed_along(value, axis, steps):
    count = lax.axis_size(axis)
    leading, last = (max(0, -steps), min(count, count - steps))
    return lax.ppermute(value, axis, [(source, source + steps) for source in range(leading, last)])


def apply_left(matrix, field):
    return jnp.einsum("jk,bkl->bjl", matrix, field, precision=lax.Precision.HIGHEST)


def apply_right(field, matrix):
    return jnp.einsum("bjk,kl->bjl", field, matrix, precision=lax.Precision.HIGHEST)


def transform(field_re, field_im, cos_table, sine_signed):
    step_re = apply_left(cos_table, field_re) - apply_left(sine_signed, field_im)
    step_im = apply_left(cos_table, field_im) + apply_left(sine_signed, field_re)
    out_re = apply_right(step_re, cos_table) - apply_right(step_im, sine_signed)
    out_im = apply_right(step_re, sine_signed) + apply_right(step_im, cos_table)
    return (out_re, out_im)


def on_device(object_field, probe_field, measured, offsets):
    probe_size = probe_field.shape[1]
    rim_width = probe_size // 2
    tile_rows = object_field.shape[1]
    tile_cols = object_field.shape[2]
    extended = extended_2(object_field, (("tile", 1), ("pos", 2)), rim_width)
    row_start = jnp.remainder(offsets[:, 0] + rim_width, tile_rows)
    col_start = jnp.remainder(offsets[:, 1] + rim_width, tile_cols)
    zero_index = jnp.int32(0)

    def take_patch(row_at, col_at):
        return lax.dynamic_slice(
            extended, (zero_index, row_at, col_at), (2, probe_size, probe_size)
        )

    patches = jax.vmap(take_patch)(row_start, col_start)
    grid = jnp.arange(probe_size, dtype=jnp.int32)
    phase = jnp.remainder(grid[:, None] * grid[None, :], probe_size).astype(jnp.float32)
    angle_table = phase * (2.0 * math.pi / probe_size)
    norm_factor = 1.0 / math.sqrt(probe_size)
    cos_table = jnp.cos(angle_table) * norm_factor
    sine_table = -jnp.sin(angle_table) * norm_factor
    patch_re = patches[:, 0]
    patch_im = patches[:, 1]
    probe_re = probe_field[0]
    probe_im = probe_field[1]
    exit_re = probe_re * patch_re - probe_im * patch_im
    exit_im = probe_re * patch_im + probe_im * patch_re
    wave_re, wave_im = transform(exit_re, exit_im, cos_table, sine_table)
    magnitude = jnp.sqrt(wave_re * wave_re + wave_im * wave_im)
    factor = 1.0 - measured / jnp.maximum(magnitude, 1.0)
    back_re, back_im = transform(wave_re * factor, wave_im * factor, cos_table, -sine_table)
    grad_re = probe_re * back_re + probe_im * back_im
    grad_im = probe_re * back_im - probe_im * back_re
    patch_grads = jnp.stack([grad_re, grad_im], axis=1)
    probe_term = jnp.stack(
        [
            jnp.sum(patch_re * back_re + patch_im * back_im, axis=0),
            jnp.sum(patch_re * back_im - patch_im * back_re, axis=0),
        ]
    )

    def add_patch(slot_id, grad_ext):
        row_at = row_start[slot_id]
        col_at = col_start[slot_id]
        current = lax.dynamic_slice(
            grad_ext, (zero_index, row_at, col_at), (2, probe_size, probe_size)
        )
        return lax.dynamic_update_slice(
            grad_ext, current + patch_grads[slot_id], (zero_index, row_at, col_at)
        )

    grad_ext = lax.fori_loop(0, offsets.shape[0], add_patch, jnp.zeros(extended.shape, jnp.float32))
    from_lower = passed_along(grad_ext[:, tile_rows + rim_width :, :], "tile", 1)
    from_upper = passed_along(grad_ext[:, :rim_width, :], "tile", -1)
    grad_ext = grad_ext.at[:, rim_width : 2 * rim_width, :].add(from_lower)
    grad_ext = grad_ext.at[:, tile_rows : tile_rows + rim_width, :].add(from_upper)
    grad_ext = grad_ext[:, rim_width : tile_rows + rim_width, :]
    from_lower = passed_along(grad_ext[:, :, tile_cols + rim_width :], "pos", 1)
    from_upper = passed_along(grad_ext[:, :, :rim_width], "pos", -1)
    grad_ext = grad_ext.at[:, :, rim_width : 2 * rim_width].add(from_lower)
    grad_ext = grad_ext.at[:, :, tile_cols : tile_cols + rim_width].add(from_upper)
    object_grad = grad_ext[:, :, rim_width : tile_cols + rim_width]
    probe_sum = lax.psum(probe_term, ("pos", "tile"))
    total_count = offsets.shape[0] * lax.axis_size("pos") * lax.axis_size("tile")
    probe_grad = probe_sum * (1.0 / math.sqrt(total_count))
    return (object_grad, probe_grad)


def solution(mesh):
    placed = (P(None, "tile", "pos"), P(), P(("pos", "tile"), None, None), P(("pos", "tile"), None))
    return jax.shard_map(
        on_device,
        mesh=mesh,
        in_specs=placed,
        out_specs=(P(None, "tile", "pos"), P()),
        check_vma=False,
    )
```

profile of v0, /device:TPU:1, one launch (start us, length us, event | category | flops | bytes accessed | tf_op | source)
XLA Modules:
  0.0 641.6 jit_solution(7473113301435112420)
XLA Ops:
  38.0 47.6 %while.19 = (s32[]{:T(128)}, f32[2,512,768]{2,1,0:T(8,128)S(1)}, s32[16,3]{0,1:T(4,128)S(1)}, f32[16,2,256,256]{3,2,0,1:T(8,128)}, s32[]{:T(128)}) while((s32[]{:T(128)}, f32[2,512,768]{2,1,0:T(8,128)S(1)}, s32[16,3]{0,1:T(4,128)S(1)}, f32[16,2,256,256]{3,2,0,1:T(8,128)}, s32[]{:T(128)}) %tuple.75), condition=%wide.while_cond.4, body=%wide.while_body.4.sunk | while | flops 2 | bytes 1050217 | solution.py:55
  85.6 11.7 %fusion.41 = f32[16,256,256]{2,1,0:T(8,128)S(1)} fusion(f32[16,2,256,256]{3,2,0,1:T(8,128)} %get-tuple-element.152, f32[256,256]{1,0:T(8,128)} %get-tuple-element.195, f32[256,256]{1,0:T(8,128)S(1)} %get-tuple-element.194), kind=kOutput, calls=%fused_computation.52 | convolution fusion | flops 3225354240 | bytes 13107200 | tf_op jit(solution)/shard_map/jk,bkl->bjl/dot_general | solution.py:29
  97.3 8.2 %fusion.37 = f32[16,256,256]{2,1,0:T(8,128)S(1)} fusion(f32[16,2,256,256]{3,2,0,1:T(8,128)S(1)} %copy-done, f32[256,256]{1,0:T(8,128)S(1)} %copy-done.2, f32[256,256]{1,0:T(8,128)S(1)} %get-tuple-element.194), kind=kOutput, calls=%fused_computation.51 | convolution fusion | flops 3225354240 | bytes 13107200 | tf_op jit(solution)/shard_map/jk,bkl->bjl/dot_general | solution.py:29
  105.4 8.7 %convolution_add_fusion.1 = f32[16,256,256]{2,1,0:T(8,128)S(1)} fusion(f32[16,256,256]{2,1,0:T(8,128)S(1)} %fusion.37, f32[16,2,256,256]{3,2,0,1:T(8,128)S(1)} %copy-done, f32[256,256]{1,0:T(8,128)S(1)} %copy-done.2, f32[256,256]{1,0:T(8,128)S(1)} %get-tuple-element.194), kind=kOutput, calls=%fused_computation.46 | convolution fusion | flops 3226468352 | bytes 17301504 | tf_op jit(solution)/shard_map/jk,bkl->bjl/dot_general | solution.py:29
  114.1 8.0 %fusion.8 = f32[16,256,256]{2,1,0:T(8,128)S(1)} fusion(f32[16,256,256]{2,1,0:T(8,128)S(1)} %convolution_add_fusion.1), kind=kOutput, calls=%fused_computation.12 | convolution fusion | flops 3222208512 | bytes 8388608 | tf_op jit(solution)/shard_map/bjk,kl->bjl/dot_general | solution.py:33
  122.1 10.6 %fusion.10 = f32[16,256,256]{2,1,0:T(8,128)} fusion(f32[16,256,256]{2,1,0:T(8,128)S(1)} %convolution_add_fusion.1), kind=kOutput, calls=%fused_computation.14 | convolution fusion | flops 3222274048 | bytes 8388608 | tf_op jit(solution)/shard_map/bjk,kl->bjl/dot_general | solution.py:33
  132.7 8.3 %convolution_subtract_fusion.1 = f32[16,256,256]{2,1,0:T(8,128)S(1)} fusion(f32[16,256,256]{2,1,0:T(8,128)S(1)} %fusion.41, f32[16,2,256,256]{3,2,0,1:T(8,128)S(1)} %copy-done, f32[256,256]{1,0:T(8,128)S(1)} %copy-done.2, f32[256,256]{1,0:T(8,128)S(1)} %get-tuple-element.194), kind=kOutput, calls=%fused_computation.47 | convolution fusion | flops 3226468352 | bytes 17301504 | tf_op jit(solution)/shard_map/jk,bkl->bjl/dot_general | solution.py:29
  141.0 8.3 %fusion.27 = f32[16,256,256]{2,1,0:T(8,128)S(1)} fusion(f32[16,256,256]{2,1,0:T(8,128)S(1)} %fusion.8, f32[16,256,256]{2,1,0:T(8,128)S(1)} %convolution_subtract_fusion.1), kind=kOutput, calls=%fused_computation.41 | convolution fusion | flops 3223322624 | bytes 12582912 | tf_op jit(solution)/shard_map/bjk,kl->bjl/dot_general | solution.py:33
  149.3 13.8 %fusion.23 = (f32[16,256,256]{2,1,0:T(8,128)S(1)}, f32[16,256,256]{2,1,0:T(8,128)S(1)}) fusion(f32[16,256,256]{2,1,0:T(8,128)} %param.16, f32[16,256,256]{2,1,0:T(8,128)S(1)} %fusion.27, f32[16,256,256]{2,1,0:T(8,128)} %fusion.10, f32[16,256,256]{2,1,0:T(8,128)S(1)} %convolution_subtract_fusion.1), kind=kOutput, calls=%fused_computation.38 | convolution fusion | flops 3231645696 | bytes 25165824 | tf_op jit(solution)/shard_map/bjk,kl->bjl/dot_general | solution.py:33
  163.1 8.1 %fusion.60 = f32[16,256,256]{2,1,0:T(8,128)S(1)} fusion(f32[16,256,256]{2,1,0:T(8,128)S(1)} %get-tuple-element.180), kind=kOutput, calls=%fused_computation.76 | convolution fusion | flops 3222208512 | bytes 8388608 | tf_op jit(solution)/shard_map/jk,bkl->bjl/dot_general | solution.py:29
  171.2 7.7 %fusion.57 = f32[16,256,256]{2,1,0:T(8,128)S(1)} fusion(f32[16,256,256]{2,1,0:T(8,128)S(1)} %get-tuple-element.181), kind=kOutput, calls=%fused_computation.73 | convolution fusion | flops 3222208512 | bytes 8388608 | tf_op jit(solution)/shard_map/jk,bkl->bjl/dot_general | solution.py:29
  178.9 8.4 %convolution_add_fusion = f32[16,256,256]{2,1,0:T(8,128)S(1)} fusion(f32[16,256,256]{2,1,0:T(8,128)S(1)} %fusion.57, f32[16,256,256]{2,1,0:T(8,128)S(1)} %get-tuple-element.180), kind=kOutput, calls=%fused_computation.44 | convolution fusion | flops 3223388160 | bytes 12582912 | tf_op jit(solution)/shard_map/jk,bkl->bjl/dot_general | solution.py:29
  187.3 7.6 %fusion = f32[16,256,256]{2,1,0:T(8,128)S(1)} fusion(f32[16,256,256]{2,1,0:T(8,128)S(1)} %convolution_add_fusion), kind=kOutput, calls=%fused_computation.4 | convolution fusion | flops 3222208512 | bytes 8388608 | tf_op jit(solution)/shard_map/bjk,kl->bjl/dot_general | solution.py:33
  194.9 8.6 %fusion.2 = f32[16,256,256]{2,1,0:T(8,128)S(1)} fusion(f32[16,256,256]{2,1,0:T(8,128)S(1)} %convolution_add_fusion), kind=kOutput, calls=%fused_computation.6 | convolution fusion | flops 3222339584 | bytes 8388608 | tf_op jit(solution)/shard_map/bjk,kl->bjl/dot_general | solution.py:33
  203.5 8.2 %convolution_subtract_fusion = f32[16,256,256]{2,1,0:T(8,128)S(1)} fusion(f32[16,256,256]{2,1,0:T(8,128)S(1)} %fusion.60, f32[16,256,256]{2,1,0:T(8,128)S(1)} %get-tuple-element.181), kind=kOutput, calls=%fused_computation.45 | convolution fusion | flops 3223388160 | bytes 12582912 | tf_op jit(solution)/shard_map/jk,bkl->bjl/dot_general | solution.py:29
  211.7 8.3 %fusion.33 = f32[16,256,256]{2,1,0:T(8,128)S(1)} fusion(f32[16,256,256]{2,1,0:T(8,128)S(1)} %fusion, f32[16,256,256]{2,1,0:T(8,128)S(1)} %convolution_subtract_fusion), kind=kOutput, calls=%fused_computation.43 | convolution fusion | flops 3223388160 | bytes 12582912 | tf_op jit(solution)/shard_map/bjk,kl->bjl/dot_general | solution.py:33
  220.0 15.9 %fusion.19 = (f32[256,256]{1,0:T(8,128)}, f32[256,256]{1,0:T(8,128)}, f32[16,1,256,256]{3,2,0,1:T(8,128)}, f32[16,1,256,256]{3,2,0,1:T(8,128)}) fusion(f32[16,256,256]{2,1,0:T(8,128)S(1)} %fusion.33, f32[16,2,256,256]{3,2,0,1:T(8,128)S(1)} %copy-done, f32[256,256]{1,0:T(8,128)} %get-tuple-element.195, f32[256,256]{1,0:T(8,128)} %copy-done.1, ...), kind=kOutput, calls=%fused_computation.27 | convolution fusion | flops 3237806080 | bytes 30408704 | tf_op jit(solution)/shard_map/bjk,kl->bjl/dot_general | solution.py:33
  235.9 7.6 %pad_maximum_fusion = f32[16,2,256,256]{3,2,0,1:T(8,128)} fusion(f32[16,1,256,256]{3,2,0,1:T(8,128)} %get-tuple-element.184, f32[16,1,256,256]{3,2,0,1:T(8,128)} %get-tuple-element.185), kind=kLoop, calls=%fused_computation.3 | loop fusion | flops 2097152 | bytes 16777216 | tf_op jit(solution)/shard_map/stack | solution.py:78
  245.4 210.0 %while.18 = (s32[]{:T(128)}, f32[2,512,768]{2,1,0:T(8,128)}, s32[16]{0:T(128)S(1)}, s32[16]{0:T(128)S(1)}, f32[16,2,256,256]{3,2,0,1:T(8,128)}, /*index=5*/s32[]{:T(128)}, s32[]{:T(128)}, s32[]{:T(128)}, s32[]{:T(128)}) while((s32[]{:T(128)}, f32[2,512,768]{2,1,0:T(8,128)}, s32[16]{0:T(128)S(1)}, s32[16]{0:T(128)S(1)}, ...), condition=%wide.region_1.2_spmd, body=%wide.region_0.1_spmd.sunk | while | flops 131080 | bytes 2621641 | solution.py:96
  252.0 6.6 %dynamic_update_slice.8 = f32[2,512,768]{2,1,0:T(8,128)} dynamic-update-slice(f32[2,512,768]{2,1,0:T(8,128)} %get-tuple-element.285, f32[2,256,256]{2,1,0:T(8,128)S(1)} %bitcast_add_fusion.2, s32[]{:T(128)} %constant.186.clone.1..sunk, s32[]{:T(128)S(6)} %select_n.164, s32[]{:T(128)S(6)} %select_n.165) | dynamic-update-slice | bytes 1048580 | tf_op jit(solution)/shard_map/while/body/eval_jaxpr/dynamic_update_slice | solution.py:92
  278.2 6.5 %dynamic_update_slice.8 = f32[2,512,768]{2,1,0:T(8,128)} dynamic-update-slice(f32[2,512,768]{2,1,0:T(8,128)} %get-tuple-element.285, f32[2,256,256]{2,1,0:T(8,128)S(1)} %bitcast_add_fusion.2, s32[]{:T(128)} %constant.186.clone.1..sunk, s32[]{:T(128)S(6)} %select_n.164, s32[]{:T(128)S(6)} %select_n.165) | dynamic-update-slice | bytes 1048580 | tf_op jit(solution)/shard_map/while/body/eval_jaxpr/dynamic_update_slice | solution.py:92
  303.9 6.8 %dynamic_update_slice.8 = f32[2,512,768]{2,1,0:T(8,128)} dynamic-update-slice(f32[2,512,768]{2,1,0:T(8,128)} %get-tuple-element.285, f32[2,256,256]{2,1,0:T(8,128)S(1)} %bitcast_add_fusion.2, s32[]{:T(128)} %constant.186.clone.1..sunk, s32[]{:T(128)S(6)} %select_n.164, s32[]{:T(128)S(6)} %select_n.165) | dynamic-update-slice | bytes 1048580 | tf_op jit(solution)/shard_map/while/body/eval_jaxpr/dynamic_update_slice | solution.py:92
  317.2 6.5 %dynamic_update_slice.8 = f32[2,512,768]{2,1,0:T(8,128)} dynamic-update-slice(f32[2,512,768]{2,1,0:T(8,128)} %get-tuple-element.285, f32[2,256,256]{2,1,0:T(8,128)S(1)} %bitcast_add_fusion.2, s32[]{:T(128)} %constant.186.clone.1..sunk, s32[]{:T(128)S(6)} %select_n.164, s32[]{:T(128)S(6)} %select_n.165) | dynamic-update-slice | bytes 1048580 | tf_op jit(solution)/shard_map/while/body/eval_jaxpr/dynamic_update_slice | solution.py:92
  343.5 6.6 %dynamic_update_slice.8 = f32[2,512,768]{2,1,0:T(8,128)} dynamic-update-slice(f32[2,512,768]{2,1,0:T(8,128)} %get-tuple-element.285, f32[2,256,256]{2,1,0:T(8,128)S(1)} %bitcast_add_fusion.2, s32[]{:T(128)} %constant.186.clone.1..sunk, s32[]{:T(128)S(6)} %select_n.164, s32[]{:T(128)S(6)} %select_n.165) | dynamic-update-slice | bytes 1048580 | tf_op jit(solution)/shard_map/while/body/eval_jaxpr/dynamic_update_slice | solution.py:92
  356.6 6.6 %dynamic_update_slice.8 = f32[2,512,768]{2,1,0:T(8,128)} dynamic-update-slice(f32[2,512,768]{2,1,0:T(8,128)} %get-tuple-element.285, f32[2,256,256]{2,1,0:T(8,128)S(1)} %bitcast_add_fusion.2, s32[]{:T(128)} %constant.186.clone.1..sunk, s32[]{:T(128)S(6)} %select_n.164, s32[]{:T(128)S(6)} %select_n.165) | dynamic-update-slice | bytes 1048580 | tf_op jit(solution)/shard_map/while/body/eval_jaxpr/dynamic_update_slice | solution.py:92
  382.9 6.6 %dynamic_update_slice.8 = f32[2,512,768]{2,1,0:T(8,128)} dynamic-update-slice(f32[2,512,768]{2,1,0:T(8,128)} %get-tuple-element.285, f32[2,256,256]{2,1,0:T(8,128)S(1)} %bitcast_add_fusion.2, s32[]{:T(128)} %constant.186.clone.1..sunk, s32[]{:T(128)S(6)} %select_n.164, s32[]{:T(128)S(6)} %select_n.165) | dynamic-update-slice | bytes 1048580 | tf_op jit(solution)/shard_map/while/body/eval_jaxpr/dynamic_update_slice | solution.py:92
  396.1 6.5 %dynamic_update_slice.8 = f32[2,512,768]{2,1,0:T(8,128)} dynamic-update-slice(f32[2,512,768]{2,1,0:T(8,128)} %get-tuple-element.285, f32[2,256,256]{2,1,0:T(8,128)S(1)} %bitcast_add_fusion.2, s32[]{:T(128)} %constant.186.clone.1..sunk, s32[]{:T(128)S(6)} %select_n.164, s32[]{:T(128)S(6)} %select_n.165) | dynamic-update-slice | bytes 1048580 | tf_op jit(solution)/shard_map/while/body/eval_jaxpr/dynamic_update_slice | solution.py:92
  409.2 6.5 %dynamic_update_slice.8 = f32[2,512,768]{2,1,0:T(8,128)} dynamic-update-slice(f32[2,512,768]{2,1,0:T(8,128)} %get-tuple-element.285, f32[2,256,256]{2,1,0:T(8,128)S(1)} %bitcast_add_fusion.2, s32[]{:T(128)} %constant.186.clone.1..sunk, s32[]{:T(128)S(6)} %select_n.164, s32[]{:T(128)S(6)} %select_n.165) | dynamic-update-slice | bytes 1048580 | tf_op jit(solution)/shard_map/while/body/eval_jaxpr/dynamic_update_slice | solution.py:92
  435.5 6.8 %dynamic_update_slice.8 = f32[2,512,768]{2,1,0:T(8,128)} dynamic-update-slice(f32[2,512,768]{2,1,0:T(8,128)} %get-tuple-element.285, f32[2,256,256]{2,1,0:T(8,128)S(1)} %bitcast_add_fusion.2, s32[]{:T(128)} %constant.186.clone.1..sunk, s32[]{:T(128)S(6)} %select_n.164, s32[]{:T(128)S(6)} %select_n.165) | dynamic-update-slice | bytes 1048580 | tf_op jit(solution)/shard_map/while/body/eval_jaxpr/dynamic_update_slice | solution.py:92
  462.8 8.9 %collective-permute-done.4 = f32[2,128,768]{2,1,0:T(8,128)S(1)} collective-permute-done((f32[2,128,768]{2,1,0:T(8,128)S(1)}, f32[2,128,768]{2,1,0:T(8,128)S(1)}, u32[]{:S(2)}, u32[]{:S(2)}) %collective-permute-start.4) | collective-permute-done | bytes 786464 | tf_op jit(solution)/shard_map/ppermute | solution.py:25
  476.9 11.3 %collective-permute-done.5 = f32[2,128,768]{2,1,0:T(8,128)S(1)} collective-permute-done((f32[2,128,768]{2,1,0:T(8,128)S(1)}, f32[2,128,768]{2,1,0:T(8,128)S(1)}, u32[]{:S(2)}, u32[]{:S(2)}) %collective-permute-start.5) | collective-permute-done | bytes 786464 | tf_op jit(solution)/shard_map/ppermute | solution.py:25
  497.7 131.2 %all-reduce.2.cloned.1.call-done = f32[2,256,256]{2,1,0:T(8,128)} async-done(((f32[2,256,256]{2,1,0:T(8,128)}), f32[2,256,256]{2,1,0:T(8,128)}) %all-reduce.2.cloned.1.call-update) | async-done | bytes 524304 | tf_op jit(solution)/shard_map/psum | solution.py:107
  (155 shorter events, 189.4 us)
Async XLA Ops:
  7.2 21.8 %copy-start.6 = (s32[16,2]{0,1:T(2,128)S(1)}, s32[16,2]{0,1:T(2,128)}, u32[]{:S(2)}) copy-start(s32[16,2]{0,1:T(2,128)} %param.17) | copy-start | bytes 388
  7.2 21.8 %copy-start.5 = (f32[2,256,256]{2,1,0:T(8,128)S(1)}, f32[2,256,256]{2,1,0:T(8,128)}, u32[]{:S(2)}) copy-start(f32[2,256,256]{2,1,0:T(8,128)} %param.15) | copy-start | bytes 1572868
  7.2 621.8 %all-reduce.2.cloned.1.call-start = ((), (), s32[]{:S(2)}) async-start(), calls=%async_computation | async-start | bytes 1048576 | tf_op jit(solution)/shard_map/psum | solution.py:107
  8.6 10.7 %collective-permute-start = (f32[2,128,512]{2,1,0:T(8,128)S(1)}, f32[2,128,512]{2,1,0:T(8,128)S(1)}, u32[]{:S(2)}, u32[]{:S(2)}) collective-permute-start(f32[2,128,512]{2,1,0:T(8,128)S(1)} %get-tuple-element.193), channel_id=1, source_target_pairs={{0,1},{1,2},{2,3},{3,4},{4,5},{5,6},{6,7},{8,9},{9,10},{10,11},{11... | collective-permute-start | bytes 1572872 | tf_op jit(solution)/shard_map/ppermute | solution.py:14
  13.2 10.5 %collective-permute-start.1 = (f32[2,128,512]{2,1,0:T(8,128)S(1)}, f32[2,128,512]{2,1,0:T(8,128)S(1)}, u32[]{:S(2)}, u32[]{:S(2)}) collective-permute-start(f32[2,128,512]{2,1,0:T(8,128)S(1)} %get-tuple-element.192), channel_id=1, source_target_pairs={{1,0},{2,1},{3,2},{4,3},{5,4},{6,5},{7,6},{9,8},{10,9},{11,10},{12... | collective-permute-start | bytes 1572872 | tf_op jit(solution)/shard_map/ppermute | solution.py:17
  23.8 10.0 %collective-permute-start.2 = (f32[2,512,128]{2,1,0:T(8,128)S(1)}, f32[2,512,128]{2,1,0:T(8,128)S(1)}, u32[]{:S(2)}, u32[]{:S(2)}) collective-permute-start(f32[2,512,128]{2,1,0:T(8,128)S(1)} %get-tuple-element.190), channel_id=1, source_target_pairs={{0,8},{8,16},{16,24},{24,32},{32,40},{40,48},{48,56},{56,64},{64,7... | collective-permute-start | bytes 1572872 | tf_op jit(solution)/shard_map/ppermute | solution.py:14
  27.7 10.1 %collective-permute-start.3 = (f32[2,512,128]{2,1,0:T(8,128)S(1)}, f32[2,512,128]{2,1,0:T(8,128)S(1)}, u32[]{:S(2)}, u32[]{:S(2)}) collective-permute-start(f32[2,512,128]{2,1,0:T(8,128)S(1)} %get-tuple-element.191), channel_id=1, source_target_pairs={{8,0},{16,8},{24,16},{32,24},{40,32},{48,40},{56,48},{64,56},{72,6... | collective-permute-start | bytes 1572872 | tf_op jit(solution)/shard_map/ppermute | solution.py:17
  29.8 102.9 %copy-start.1 = (f32[256,256]{1,0:T(8,128)}, f32[256,256]{1,0:T(8,128)S(1)}, u32[]{:S(2)}) copy-start(f32[256,256]{1,0:T(8,128)S(1)} %get-tuple-element.194) | copy-start | bytes 786436
  85.6 11.7 %copy-start = (f32[16,2,256,256]{3,2,0,1:T(8,128)S(1)}, f32[16,2,256,256]{3,2,0,1:T(8,128)}, u32[]{:S(2)}) copy-start(f32[16,2,256,256]{3,2,0,1:T(8,128)} %get-tuple-element.152) | copy-start | bytes 25165828
  85.6 11.7 %copy-start.2 = (f32[256,256]{1,0:T(8,128)S(1)}, f32[256,256]{1,0:T(8,128)}, u32[]{:S(2)}) copy-start(f32[256,256]{1,0:T(8,128)} %get-tuple-element.195) | copy-start | bytes 786436
  455.4 20.6 %copy-start.3 = (f32[256,256]{1,0:T(8,128)S(1)}, f32[256,256]{1,0:T(8,128)}, u32[]{:S(2)}) copy-start(f32[256,256]{1,0:T(8,128)} %get-tuple-element.158) | copy-start | bytes 786436
  455.4 20.6 %copy-start.4 = (f32[256,256]{1,0:T(8,128)S(1)}, f32[256,256]{1,0:T(8,128)}, u32[]{:S(2)}) copy-start(f32[256,256]{1,0:T(8,128)} %get-tuple-element.159) | copy-start | bytes 786436
  456.7 15.0 %collective-permute-start.4 = (f32[2,128,768]{2,1,0:T(8,128)S(1)}, f32[2,128,768]{2,1,0:T(8,128)S(1)}, u32[]{:S(2)}, u32[]{:S(2)}) collective-permute-start(f32[2,128,768]{2,1,0:T(8,128)S(1)} %slice.158), channel_id=1, source_target_pairs={{0,1},{1,2},{2,3},{3,4},{4,5},{5,6},{6,7},{8,9},{9,10},{10,11},{11... | collective-permute-start | bytes 2359304 | tf_op jit(solution)/shard_map/ppermute | solution.py:25
  474.1 14.0 %collective-permute-start.5 = (f32[2,128,768]{2,1,0:T(8,128)S(1)}, f32[2,128,768]{2,1,0:T(8,128)S(1)}, u32[]{:S(2)}, u32[]{:S(2)}) collective-permute-start(f32[2,128,768]{2,1,0:T(8,128)S(1)} %get-tuple-element.188), channel_id=1, source_target_pairs={{1,0},{2,1},{3,2},{4,3},{5,4},{6,5},{7,6},{9,8},{10,9},{11,10},{12... | collective-permute-start | bytes 2359304 | tf_op jit(solution)/shard_map/ppermute | solution.py:25
  491.3 141.0 %collective-permute-start.6 = (f32[2,256,128]{2,1,0:T(8,128)S(1)}, f32[2,256,128]{2,1,0:T(8,128)S(1)}, u32[]{:S(2)}, u32[]{:S(2)}) collective-permute-start(f32[2,256,128]{2,1,0:T(8,128)S(1)} %get-tuple-element.187), channel_id=1, source_target_pairs={{0,8},{8,16},{16,24},{24,32},{32,40},{40,48},{48,56},{56,64},{64,7... | collective-permute-start | bytes 786440 | tf_op jit(solution)/shard_map/ppermute | solution.py:25
  496.4 136.9 %collective-permute-start.7 = (f32[2,256,128]{2,1,0:T(8,128)S(1)}, f32[2,256,128]{2,1,0:T(8,128)S(1)}, u32[]{:S(2)}, u32[]{:S(2)}) collective-permute-start(f32[2,256,128]{2,1,0:T(8,128)S(1)} %get-tuple-element.186), channel_id=1, source_target_pairs={{8,0},{16,8},{24,16},{32,24},{40,32},{48,40},{56,48},{64,56},{72,6... | collective-permute-start | bytes 786440 | tf_op jit(solution)/shard_map/ppermute | solution.py:25
Sparse Core Ops, SparseCore 0:
  477.0 151.9 all-reduce.1
where the time goes:
time: 651 us; the launch traced here: 642 us
  local copies, waits for them, and re-layouts  181 us (28%)
  waiting for transfers between devices  166 us (25%)
  matrix products  150 us (23%)
  loops' own time  62.3 us (10%)
  other arithmetic  41.4 us (6%)
  starting transfers between devices  26.1 us (4%)
  between operations  14.6 us (2%)
    psum x1, waiting for transfers between devices, on_device(): probe_sum = lax.psum(probe_term, ('pos', 'tile'))  131 us
    dynamic_update_slice x16, local copies, waits for them, and re-layouts, add_patch(): lax.dynamic_update_slice(grad_ext, current + patch_grads[slot_id], (zero_...  104 us
    dot_general x8, matrix products, apply_right(): jnp.einsum('bjk,kl->bjl', field, matrix, precision=lax.Precision.HIGHEST)  81 us
    dot_general x8, matrix products, apply_left(): jnp.einsum('jk,bkl->bjl', matrix, field, precision=lax.Precision.HIGHEST)  69.2 us
    another operation x1, loops' own time, on_device(): lax.fori_loop(0, offsets.shape[0], add_patch, jnp.zeros(extended.shape, j...  62.3 us
    gather x48, local copies, waits for them, and re-layouts  47.6 us
    add x16, other arithmetic, add_patch(): current + patch_grads[slot_id]  24.5 us
    ppermute x4, waiting for transfers between devices, passed_along(): lax.ppermute(value, axis, [(source, source + steps) for source in range(l...  20.2 us
  transfers between devices with their start and end apart: 9, of which 7 were waited for; matrix products, arithmetic and copies ran while one was open for 2% of the time, Pallas kernels for 0%

commit v1 on v0

v1 whole, which is shorter than its diff:
```python
import functools
import math

import jax
import jax.numpy as jnp
import numpy as np
from jax import lax
from jax.experimental import pallas as pl
from jax.experimental.pallas import tpu as pltpu
from jax.sharding import PartitionSpec as P

LANES = 128
RIM = 128
F32 = jnp.float32
BF16 = jnp.bfloat16
MESH = pl.DeviceIdType.MESH


def dft_tables(size):
    half = size // 2
    n = np.arange(half)[:, None]
    k = np.arange(half)[None, :]
    out = []
    for parity in range(2):
        phase = (n * (2 * k + parity)) % size
        table = np.exp(-2j * np.pi * phase / size) / math.sqrt(size)
        real = np.block([[table.real, table.imag], [-table.imag, table.real]])
        out += [real, real.T]
    stack = np.stack(out)
    high = stack.astype(np.float32).astype(BF16)
    low = (stack - high.astype(np.float64)).astype(np.float32).astype(BF16)
    return np.stack([high, low], axis=1)


def orderings(size):
    order = np.concatenate([np.arange(0, size, 2), np.arange(1, size, 2)])
    rows = np.zeros((size, size), np.float32)
    rows[np.arange(size), order] = 1.0
    return np.stack([rows, rows.T]).astype(BF16)


def split(value):
    high = value.astype(BF16)
    return high, (value - high.astype(F32)).astype(BF16)


def dot(a, b):
    return jnp.dot(a, b, preferred_element_type=F32)


def cat(parts, axis):
    return tuple(jnp.concatenate(p, axis=axis) for p in zip(*parts))


def one_position(chunk, row, col, meas, ext_ref, probe_ref, tab_ref, acc_ref, term_ref, rolled):
    size, half = 256, 128
    lane = lax.broadcasted_iota(jnp.int32, (chunk, LANES), 1)
    block = col // LANES
    shift = lax.rem(col, LANES)
    mask = lane >= shift

    def patch(start):
        rows = pl.ds(row + start, chunk)
        out = []
        for plane in range(2):
            b0 = ext_ref[plane, block, rows, :]
            b1 = ext_ref[plane, block + 1, rows, :]
            b2 = ext_ref[plane, block + 2, rows, :]
            out.append((jnp.where(mask, b0, b2), b1))
        return out

    sums, diffs = [], []
    for start in range(0, size, chunk):
        rows = pl.ds(start, chunk)
        (x0r, x1r), (x0i, x1i) = patch(start)
        pr = []
        for plane in range(2):
            r0 = pltpu.roll(probe_ref[plane, 0, rows, :], shift, 1)
            r1 = pltpu.roll(probe_ref[plane, 1, rows, :], shift, 1)
            p0 = jnp.where(mask, r0, r1)
            p1 = jnp.where(mask, r1, r0)
            rolled[plane, 0, rows, :] = p0
            rolled[plane, 1, rows, :] = p1
            pr.append((p0, p1))
        (p0r, p1r), (p0i, p1i) = pr
        e0r = p0r * x0r - p0i * x0i
        e0i = p0r * x0i + p0i * x0r
        e1r = p1r * x1r - p1i * x1i
        e1i = p1r * x1i + p1i * x1r
        sums.append(cat([split(e0r + e1r), split(e0i + e1i)], 1))
        diffs.append(cat([split(e0r - e1r), split(e0i - e1i)], 1))
    a, b = cat(sums, 0), cat(diffs, 0)

    def right(data, index):
        t = tab_ref[index, 0]
        return dot(data[0], t) + dot(data[1], t) + dot(data[0], tab_ref[index, 1])

    def left(index, data):
        t = tab_ref[index, 0]
        return dot(t, data[0]) + dot(t, data[1]) + dot(tab_ref[index, 1], data[0])

    yield
    ye = right(a, 0)
    yo = right(b, 2)
    yield
    s = [y[:half] + y[half:] for y in (ye, yo)]
    d = [y[:half] - y[half:] for y in (ye, yo)]
    a, b = [cat([cat([split(v[:, :LANES]) for v in w], 1), cat([split(v[:, LANES:]) for v in w], 1)], 0)
            for w in (s, d)]
    yield
    ze = left(1, a)
    zo = left(3, b)
    yield
    outs = []
    for z, first in ((ze, 0), (zo, half)):
        zr, zi = z[:half], z[half:]
        power = zr * zr + zi * zi
        factor = 1.0 - meas[pl.ds(first, half), :] * lax.rsqrt(jnp.maximum(power, 1.0))
        outs.append(cat([split(zr * factor), split(zi * factor)], 0))
    a, b = outs
    yield
    e = left(0, a)
    o = left(2, b)
    yield
    s, d = e + o, e - o
    a, b = [cat([cat([split(v[:half, cols]), split(v[half:, cols])], 1) for v in (s, d)], 0)
            for cols in (slice(0, LANES), slice(LANES, 2 * LANES))]
    yield
    e = right(a, 1)
    o = right(b, 3)
    yield
    back_shift = lax.rem(LANES - shift, LANES)
    keep = lane < LANES - shift
    for start in range(0, size, chunk):
        rows = pl.ds(start, chunk)
        ee, oo = e[start:start + chunk], o[start:start + chunk]
        b0, b1 = ee + oo, ee - oo
        b0r, b0i = b0[:, :LANES], b0[:, LANES:]
        b1r, b1i = b1[:, :LANES], b1[:, LANES:]
        p0r, p1r = rolled[0, 0, rows, :], rolled[0, 1, rows, :]
        p0i, p1i = rolled[1, 0, rows, :], rolled[1, 1, rows, :]
        grads = ((p0r * b0r + p0i * b0i, p1r * b1r + p1i * b1i),
                 (p0r * b0i - p0i * b0r, p1r * b1i - p1i * b1r))
        (x0r, x1r), (x0i, x1i) = patch(start)
        dst = pl.ds(row + start, chunk)
        for plane, (g0, g1) in enumerate(grads):
            acc_ref[plane, block, dst, :] += jnp.where(mask, g0, 0.0)
            acc_ref[plane, block + 1, dst, :] += g1
            acc_ref[plane, block + 2, dst, :] += jnp.where(mask, 0.0, g0)
        terms = ((x0r * b0r + x0i * b0i, x1r * b1r + x1i * b1i),
                 (x0r * b0i - x0i * b0r, x1r * b1i - x1i * b1r))
        for plane, (t0, t1) in enumerate(terms):
            r0 = pltpu.roll(t0, back_shift, 1)
            r1 = pltpu.roll(t1, back_shift, 1)
            term_ref[plane, 0, rows, :] += jnp.where(keep, r0, r1)
            term_ref[plane, 1, rows, :] += jnp.where(keep, r1, r0)


def compute_kernel(per_step, chunk, stagger, off_ref, ext_ref, probe_ref, meas_ref, tab_ref,
                   acc_ref, term_ref, rolled):
    step = pl.program_id(0)

    @pl.when(step == 0)
    def _():
        acc_ref[...] = jnp.zeros_like(acc_ref)
        term_ref[...] = jnp.zeros_like(term_ref)

    live = []
    for slot in range(per_step):
        pos = step * per_step + slot
        row = lax.rem(off_ref[pos, 0] + 128, 256)
        col = lax.rem(off_ref[pos, 1] + 128, 512)
        live.append(one_position(chunk, row, col, meas_ref.at[slot], ext_ref, probe_ref, tab_ref,
                                 acc_ref, term_ref, rolled.at[slot]))
    stages = 9
    for tick in range(stages + stagger * (per_step - 1)):
        for slot, gen in enumerate(live):
            if 0 <= tick - stagger * slot < stages:
                next(gen, None)


def compute(offsets, ext, probe, meas, tables, per_step=1, chunk=32, stagger=1):
    count = offsets.shape[0]
    whole = lambda a: pl.BlockSpec(a.shape, lambda i: (0,) * a.ndim)
    return pl.pallas_call(
        functools.partial(compute_kernel, per_step, chunk, stagger),
        grid=(count // per_step,),
        in_specs=[
            pl.BlockSpec(memory_space=pltpu.SMEM),
            whole(ext), whole(probe),
            pl.BlockSpec((per_step, 256, 256), lambda i: (i, 0, 0)),
            whole(tables),
        ],
        out_specs=[whole(ext), whole(probe)],
        out_shape=[jax.ShapeDtypeStruct(ext.shape, F32), jax.ShapeDtypeStruct(probe.shape, F32)],
        scratch_shapes=[pltpu.VMEM((per_step, 2, 2, 256, 128), F32)],
        compiler_params=pltpu.CompilerParams(vmem_limit_bytes=48 * 2**20),
        name="updates",
    )(offsets, ext, probe, meas, tables)


POS, TILE = "pos", "tile"
DIRECTIONS = tuple((dy, dx) for dy in (-1, 0, 1) for dx in (-1, 0, 1) if (dy, dx) != (0, 0))


def neighbour(dy, dx):
    p, t = lax.axis_index(POS), lax.axis_index(TILE)
    tp, tt = p + dx, t + dy
    inside = (tp >= 0) & (tp < lax.axis_size(POS)) & (tt >= 0) & (tt < lax.axis_size(TILE))
    return (tp, tt), inside


def region(dy, dx):
    rows = {-1: (0, RIM), 0: (RIM, 2 * RIM), 1: (3 * RIM, RIM)}[dy]
    blocks = {-1: (0, 1), 0: (1, 4), 1: (5, 1)}[dx]
    return rows, blocks


def greet(peers):
    barrier = pltpu.get_barrier_semaphore()
    for device, inside in peers:
        @pl.when(inside)
        def _():
            pl.semaphore_signal(barrier, inc=1, device_id=device, device_id_type=MESH)
    pl.semaphore_wait(barrier, sum(inside.astype(jnp.int32) for _, inside in peers))


def halo_kernel(obj_ref, meas_ref, perm_ref, ext_ref, out_ref, zeros, loaded, ordered, send_sem, recv_sem,
                fill_sem, own_sem, in_sem, out_sem):
    group = loaded.shape[0] // in_sem.shape[0]
    size = loaded.shape[1]
    loads = [pltpu.make_async_copy(meas_ref.at[pl.ds(g * group, group)], loaded.at[pl.ds(g * group, group)], in_sem.at[g])
             for g in range(in_sem.shape[0])]
    owns = [pltpu.make_async_copy(obj_ref.at[:, :, pl.ds(b * LANES, LANES)], ext_ref.at[:, b + 1, pl.ds(RIM, 2 * RIM), :],
                                  own_sem.at[b]) for b in range(4)]
    peers = [neighbour(*d) for d in DIRECTIONS]
    greet(peers)
    copies = []
    index = 0
    for (dy, dx), (device, inside) in zip(DIRECTIONS, peers):
        src_row, count = {-1: (0, RIM), 0: (0, 2 * RIM), 1: (RIM, RIM)}[dy]
        for b in {-1: (0,), 0: range(4), 1: (3,)}[dx]:
            (dst_row, _), (first, _) = region(-dy, -dx)
            dst_block = first + (b if dx == 0 else 0)
            copy = pltpu.make_async_remote_copy(
                src_ref=obj_ref.at[:, pl.ds(src_row, count), pl.ds(b * LANES, LANES)],
                dst_ref=ext_ref.at[:, dst_block, pl.ds(dst_row, count), :],
                send_sem=send_sem.at[index], recv_sem=recv_sem.at[index],
                device_id=device, device_id_type=MESH)
            _, from_inside = neighbour(-dy, -dx)
            fill = pltpu.make_async_copy(zeros.at[:, pl.ds(0, count), :],
                                         ext_ref.at[:, dst_block, pl.ds(dst_row, count), :], fill_sem.at[index])
            copies.append((copy, inside, from_inside, fill))
            index += 1

            @pl.when(inside)
            def _():
                copy.start()
    for load in loads:
        load.start()
    for own in owns:
        own.start()
    zeros[...] = jnp.zeros_like(zeros)
    for copy, inside, from_inside, fill in copies:
        @pl.when(jnp.logical_not(from_inside))
        def _():
            fill.start()
    perm_rows, perm_cols = perm_ref[0], perm_ref[1]
    stores = []
    for g in range(in_sem.shape[0]):
        loads[g].wait()

        def order(i, carry):
            at = g * group + 2 * i
            parts = [split(loaded[at + j]) for j in range(2)]
            done = None
            for k in range(2):
                rows = jnp.concatenate([parts[0][k], parts[1][k]], axis=0)
                moved = dot(rows, perm_cols).astype(BF16)
                moved = jnp.concatenate([moved[:size], moved[size:]], axis=1)
                moved = dot(perm_rows, moved)
                done = moved if done is None else done + moved
            ordered[at] = done[:, :size]
            ordered[at + 1] = done[:, size:]
            return carry

        lax.fori_loop(0, group // 2, order, 0)
        store = pltpu.make_async_copy(ordered.at[pl.ds(g * group, group)], out_ref.at[pl.ds(g * group, group)], out_sem.at[g])
        store.start()
        stores.append(store)
    for store in stores:
        store.wait()
    for own in owns:
        own.wait()
    for copy, inside, from_inside, fill in copies:
        @pl.when(inside)
        def _():
            copy.wait_send()

        @pl.when(from_inside)
        def _():
            copy.wait_recv()

        @pl.when(jnp.logical_not(from_inside))
        def _():
            fill.wait()


def exchange(object_field, measured, perms):
    count, size = measured.shape[0], measured.shape[1]
    groups = 4
    return pl.pallas_call(
        halo_kernel,
        in_specs=[pl.BlockSpec(memory_space=pl.ANY), pl.BlockSpec(memory_space=pl.ANY), pl.BlockSpec(memory_space=pltpu.VMEM)],
        out_specs=[pl.BlockSpec(memory_space=pl.ANY)] * 2,
        out_shape=[jax.ShapeDtypeStruct((2, 6, 4 * RIM, LANES), F32), jax.ShapeDtypeStruct(measured.shape, F32)],
        scratch_shapes=[
            pltpu.VMEM((2, 2 * RIM, LANES), F32),
            pltpu.VMEM(measured.shape, F32),
            pltpu.VMEM(measured.shape, F32),
            pltpu.SemaphoreType.DMA((14,)), pltpu.SemaphoreType.DMA((14,)), pltpu.SemaphoreType.DMA((14,)),
            pltpu.SemaphoreType.DMA((4,)), pltpu.SemaphoreType.DMA((groups,)), pltpu.SemaphoreType.DMA((groups,)),
        ],
        compiler_params=pltpu.CompilerParams(collective_id=0, has_side_effects=True, vmem_limit_bytes=40 * 2**20),
        name="halo",
    )(object_field, measured, perms)


def gather_kernel(acc_ref, term_ref, obj_ref, probe_ref, own, total, result, *rest):
    (recv_v, recv_h, recv_d, part1, part2, part3,
     load_sem, send_sem, recv_sem, s1, r1, s2, r2, s3, r3, s4, r4, s5, r5, s6, r6, out_sem, pout_sem) = rest
    p, t = lax.axis_index(POS), lax.axis_index(TILE)
    x, z = p // 4, lax.rem(p, 4)
    y, core = t // 2, lax.rem(t, 2)
    yz = y * 4 + z
    yes = p >= 0
    partner = (p, t + 1 - 2 * core)
    x_peers = [(lax.rem(x + k, 4) * 4 + z, t) for k in range(1, 4)]
    x_ids = [lax.rem(x + k, 4) for k in range(1, 4)]
    yz_ids = [lax.rem(yz + k, 16) for k in range(1, 16)]
    yz_peers = [(x * 4 + lax.rem(i, 4), (i // 4) * 2 + core) for i in yz_ids]
    around = [neighbour(*d) for d in DIRECTIONS]

    load_total = pltpu.make_async_copy(term_ref, total, load_sem.at[0])
    load_own = pltpu.make_async_copy(acc_ref.at[:, pl.ds(1, 4), pl.ds(RIM, 2 * RIM), :], own, load_sem.at[1])
    load_total.start()
    load_own.start()
    greet(around + [(partner, yes)] + [(d, yes) for d in x_peers] + [(d, yes) for d in yz_peers])

    def remote(src, dst, send, recv, device):
        return pltpu.make_async_remote_copy(src_ref=src, dst_ref=dst, send_sem=send, recv_sem=recv,
                                            device_id=device, device_id_type=MESH)

    load_total.wait()
    half = 512
    mine = pl.multiple_of(core * half, half)
    other = pl.multiple_of((1 - core) * half, half)
    first = remote(total.at[pl.ds(other, half)], part1, s1, r1, partner)
    first.start()
    copies = []
    for index, ((dy, dx), (device, inside)) in enumerate(zip(DIRECTIONS, around)):
        (row, rows), (block, blocks) = region(dy, dx)
        slot = {-1: 0, 1: 1}
        if dx == 0:
            dst = recv_v.at[slot[dy]]
        elif dy == 0:
            dst = recv_h.at[slot[dx]]
        else:
            dst = recv_d.at[slot[dy] * 2 + slot[dx]]
        copy = remote(acc_ref.at[:, pl.ds(block, blocks), pl.ds(row, rows), :], dst, send_sem.at[index], recv_sem.at[index], device)
        _, from_inside = neighbour(-dy, -dx)
        copies.append((copy, inside, from_inside, dst, dy, dx))

        @pl.when(inside)
        def _():
            copy.start()
    first.wait()
    total[pl.ds(mine, half)] = total[pl.ds(mine, half)] + part1[...]
    quarter = half // 4
    seconds = [remote(total.at[pl.ds(pl.multiple_of(mine + i * quarter, quarter), quarter)], part2.at[k], s2.at[k], r2.at[k], d)
               for k, (i, d) in enumerate(zip(x_ids, x_peers))]
    for c in seconds:
        c.start()
    load_own.wait()
    for c in seconds:
        c.wait()
    at2 = pl.multiple_of(mine + x * quarter, quarter)
    total[pl.ds(at2, quarter)] = total[pl.ds(at2, quarter)] + part2[0] + part2[1] + part2[2]
    piece = quarter // 16
    thirds = [remote(total.at[pl.ds(pl.multiple_of(at2 + i * piece, piece), piece)], part3.at[k], s3.at[k], r3.at[k], d)
              for k, (i, d) in enumerate(zip(yz_ids, yz_peers))]
    for c in thirds:
        c.start()
    for c in thirds:
        c.wait()
    at3 = pl.multiple_of(at2 + yz * piece, piece)
    value = total[pl.ds(at3, piece)]
    for k in range(15):
        value = value + part3[k]
    result[pl.ds(at3, piece)] = value * (1.0 / math.sqrt(2048))
    here = result.at[pl.ds(at3, piece)]
    fourths = [remote(here, here, s4.at[k], r4.at[k], d) for k, d in enumerate(yz_peers)]
    for c in fourths:
        c.start()
    outs = []
    for copy, inside, from_inside, dst, dy, dx in copies:
        to_row, to_rows = {-1: (RIM, RIM), 0: (0, 2 * RIM), 1: (0, RIM)}[dy]
        to_block, blocks = {-1: (3, 1), 0: (0, 4), 1: (0, 1)}[dx]

        @pl.when(from_inside)
        def _():
            copy.wait_recv()
            def add(i, carry):
                b = i // 2
                rows = pl.ds(to_row, to_rows)
                own[lax.rem(i, 2), to_block + b, rows, :] = own[lax.rem(i, 2), to_block + b, rows, :] + dst[lax.rem(i, 2), b]
                return carry
            lax.fori_loop(0, 2 * blocks, add, 0)

        @pl.when(inside)
        def _():
            copy.wait_send()
    for b in range(4):
        out = pltpu.make_async_copy(own.at[:, b], obj_ref.at[:, :, pl.ds(b * LANES, LANES)], out_sem.at[b])
        out.start()
        outs.append(out)
    for c in fourths:
        c.wait()
    here2 = result.at[pl.ds(at2, quarter)]
    fifths = [remote(here2, here2, s5.at[k], r5.at[k], d) for k, d in enumerate(x_peers)]
    for c in fifths:
        c.start()
    for c in fifths:
        c.wait()
    here1 = result.at[pl.ds(mine, half)]
    last = remote(here1, here1, s6, r6, partner)
    last.start()
    last.wait()
    for i in range(4):
        out = pltpu.make_async_copy(result.at[pl.ds(i * 256, 256)], probe_ref.at[i // 2, :, pl.ds((i % 2) * LANES, LANES)], pout_sem.at[i])
        out.start()
        outs.append(out)
    for out in outs:
        out.wait()


def collect(acc, term):
    dma = pltpu.SemaphoreType.DMA
    return pl.pallas_call(
        gather_kernel,
        in_specs=[pl.BlockSpec(memory_space=pl.ANY)] * 2,
        out_specs=[pl.BlockSpec(memory_space=pl.ANY)] * 2,
        out_shape=[jax.ShapeDtypeStruct((2, 256, 512), F32), jax.ShapeDtypeStruct((2, 256, 256), F32)],
        scratch_shapes=[
            pltpu.VMEM((2, 4, 2 * RIM, LANES), F32),
            pltpu.VMEM((1024, LANES), F32),
            pltpu.VMEM((1024, LANES), F32),
            pltpu.VMEM((2, 2, 4, RIM, LANES), F32),
            pltpu.VMEM((2, 2, 1, 2 * RIM, LANES), F32),
            pltpu.VMEM((4, 2, 1, RIM, LANES), F32),
            pltpu.VMEM((512, LANES), F32),
            pltpu.VMEM((3, 128, LANES), F32),
            pltpu.VMEM((15, 8, LANES), F32),
            dma((2,)), dma((8,)), dma((8,)), dma, dma, dma((3,)), dma((3,)), dma((15,)), dma((15,)),
            dma((15,)), dma((15,)), dma((3,)), dma((3,)), dma, dma, dma((4,)), dma((4,)),
        ],
        compiler_params=pltpu.CompilerParams(collective_id=1, has_side_effects=True, vmem_limit_bytes=40 * 2**20),
        name="collect",
    )(acc, term.reshape(1024, LANES))


def on_device(object_field, probe_field, measured, offsets):
    ext, ordered = exchange(object_field, measured, jnp.asarray(orderings(256)))
    probe = jnp.stack([probe_field[:, :, :LANES], probe_field[:, :, LANES:]], axis=1)
    acc, term = compute(offsets, ext, probe, ordered, jnp.asarray(dft_tables(256)), per_step=2)
    return collect(acc, term)


def solution(mesh):
    placed = (P(None, "tile", "pos"), P(), P(("pos", "tile"), None, None), P(("pos", "tile"), None))
    return jax.shard_map(
        on_device,
        mesh=mesh,
        in_specs=placed,
        out_specs=(P(None, "tile", "pos"), P()),
        check_vma=False,
    )
```

time: 651 us -> 94.6 us (0.15); the launches traced: 642 us -> 94.3 us
  local copies, waits for them, and re-layouts: 181 us -> 11.6 us
  waiting for transfers between devices: 166 us -> 0 us
  matrix products: 150 us -> 0 us
  Pallas kernels: 0 us -> 82 us
  loops' own time: 62.3 us -> 0 us
  other arithmetic: 41.4 us -> 0.04 us
  starting transfers between devices: 26.1 us -> 0 us
  between operations: 14.6 us -> 0.69 us
    dot_general x16 -> x0, matrix products: 150 us -> none  [the longest x8 81 us: apply_right(): jnp.einsum('bjk,kl->bjl', field, matrix, precision=lax.Precision.HIGHEST)]
    psum x1 -> x0, waiting for transfers between devices: 131 us -> none  [on_device(): probe_sum = lax.psum(probe_term, ('pos', 'tile'))]
    dynamic_update_slice x16 -> x0, local copies, waits for them, and re-layouts: 104 us -> none  [add_patch(): lax.dynamic_update_slice(grad_ext, current + patch_grads[slot_id], (zero_...]
    pallas_call x0 -> x3, Pallas kernels: none -> 82 us  [the longest x1 43 us: collect(): pl.pallas_call(gather_kernel, in_specs=[pl.BlockSpec(memory_space=pl.ANY)...]
    another operation x2 -> x0, loops' own time: 62.3 us -> none  [the longest x1 62.3 us: on_device(): lax.fori_loop(0, offsets.shape[0], add_patch, jnp.zeros(extended.shape, j...]
    gather x48 -> x0, local copies, waits for them, and re-layouts: 47.6 us -> none
    ppermute x8 -> x0, waiting for transfers between devices: 34.6 us -> none  [the longest x4 20.2 us: passed_along(): lax.ppermute(value, axis, [(source, source + steps) for source in range(l...]
    ppermute x8 -> x0, starting transfers between devices: 26.1 us -> none  [the longest x4 14.4 us: passed_along(): lax.ppermute(value, axis, [(source, source + steps) for source in range(l...]
  transfers between devices with their start and end apart: 9 -> 0, of which waited for: 7 -> 0; matrix products, arithmetic and copies ran while one was open for 2% -> 0% of each run, Pallas kernels for 0% -> 0%
where the time goes in v1:
time: 94.6 us; the launch traced here: 94.3 us
  Pallas kernels  82 us (87%)
  local copies, waits for them, and re-layouts  11.6 us (12%)
    pallas_call x1, Pallas kernels, collect(): pl.pallas_call(gather_kernel, in_specs=[pl.BlockSpec(memory_space=pl.ANY)...  43 us
    pallas_call x1, Pallas kernels, compute(): pl.pallas_call(functools.partial(compute_kernel, per_step, chunk, stagger...  22.4 us
    pallas_call x1, Pallas kernels, exchange(): pl.pallas_call(halo_kernel, in_specs=[pl.BlockSpec(memory_space=pl.ANY),...  16.5 us
    unnamed x15, local copies, waits for them, and re-layouts  10.6 us

profile of v1, /device:TPU:1, one launch (start us, length us, event | category | flops | bytes accessed | tf_op | source)
XLA Modules:
  0.0 94.3 jit_solution(15980130143302584813)
XLA Ops:
  0.6 0.0 copy-start.3
  0.6 0.8 copy.8.off_ref
  1.5 1.1 %slice_bitcast_fusion.1 = (f32[2,1,256,128]{3,2,1,0:T(8,128)S(1)}, f32[2,1,256,128]{3,2,1,0:T(8,128)S(1)}) fusion(f32[2,256,256]{2,1,0:T(8,128)} %param.7), kind=kLoop, calls=%fused_computation.2 | loop fusion | bytes 1048576 | tf_op jit(solution)/shard_map/stack | solution.py:474
  2.6 0.0 copy-start.1
  2.6 2.2 %copy-done.1 = f32[16,256,256]{2,1,0:T(8,128)S(1)} copy-done((f32[16,256,256]{2,1,0:T(8,128)S(1)}, f32[16,256,256]{2,1,0:T(8,128)}, u32[]{:S(2)}) %copy-start.1) | copy-done | bytes 4194328
  4.8 0.0 copy-start.4
  4.8 1.2 %copy-done.4 = f32[2,256,512]{2,1,0:T(8,128)S(1)} copy-done((f32[2,256,512]{2,1,0:T(8,128)S(1)}, f32[2,256,512]{2,1,0:T(8,128)}, u32[]{:S(2)}) %copy-start.4) | copy-done | bytes 1048600
  6.0 0.0 copy-start.5
  6.0 0.9 %copy-done.5 = bf16[2,256,256]{2,1,0:T(8,128)(2,1)S(1)} copy-done((bf16[2,256,256]{2,1,0:T(8,128)(2,1)S(1)}, bf16[2,256,256]{2,1,0:T(8,128)(2,1)}, u32[]{:S(2)}) %copy-start.5) | copy-done | bytes 262168
  7.0 16.5 %halo.1 = (f32[2,6,512,128]{3,2,1,0:T(8,128)S(1)}, f32[16,256,256]{2,1,0:T(8,128)S(1)}) custom-call(f32[2,256,512]{2,1,0:T(8,128)S(1)} %copy-done.4, f32[16,256,256]{2,1,0:T(8,128)S(1)} %copy-done.1, bf16[2,256,256]{2,1,0:T(8,128)(2,1)S(1)} %copy-done.5), custom_call_target="tpu_custom_call" | custom-call | tf_op jit(solution)/shard_map/halo/pallas_call | solution.py:312
  23.5 0.0 copy-start
  23.5 1.9 %copy-done = f32[16,256,256]{2,1,0:T(8,128)} copy-done((f32[16,256,256]{2,1,0:T(8,128)}, f32[16,256,256]{2,1,0:T(8,128)S(1)}, u32[]{:S(2)}) %copy-start) | copy-done | bytes 4194328
  25.4 0.0 copy-start.2
  25.4 1.7 %copy-done.2 = f32[2,6,512,128]{3,2,1,0:T(8,128)} copy-done((f32[2,6,512,128]{3,2,1,0:T(8,128)}, f32[2,6,512,128]{3,2,1,0:T(8,128)S(1)}, u32[]{:S(2)}) %copy-start.2) | copy-done | bytes 3145752
  27.1 0.0 copy-done.3
  27.1 22.4 %updates.1 = (f32[2,6,512,128]{3,2,1,0:T(8,128)S(1)}, f32[2,2,256,128]{3,2,1,0:T(8,128)S(1)}) custom-call(s32[16,2]{1,0:T(8,128)S(1)} %copy.8.off_ref, f32[2,6,512,128]{3,2,1,0:T(8,128)} %copy-done.2, f32[2,2,256,128]{3,2,1,0:T(8,128)S(1)} %pad_maximum_fusion.probe_ref, f32[16,256,256]{2,1,0:T(8,128)} %copy-done, bf16[4,2,256,256]{3,2,1,0:T(8,128)(2,1)S(1)} %copy-done.3), custom_call_target="tpu_custom_call" | custom-call | tf_op jit(solution)/shard_map/updates/pallas_call | solution.py:185
  49.5 43.0 %collect.1 = (f32[2,256,512]{2,1,0:T(8,128)S(1)}, f32[2,256,256]{2,1,0:T(8,128)S(1)}) custom-call(f32[2,6,512,128]{3,2,1,0:T(8,128)S(1)} %get-tuple-element.8.acc_ref, f32[1024,128]{1,0:T(8,128)S(1)} %bitcast.5), custom_call_target="tpu_custom_call" | custom-call | tf_op jit(solution)/shard_map/collect/pallas_call | solution.py:449
  92.6 1.0 %copy.11 = f32[2,256,512]{2,1,0:T(8,128)} copy(f32[2,256,512]{2,1,0:T(8,128)S(1)} %get-tuple-element.14) | data formatting | bytes 2097152
  93.6 0.8 copy.12
  (1 shorter events, 0.0 us)
Async XLA Ops:
  0.6 26.5 %copy-start.3 = (bf16[4,2,256,256]{3,2,1,0:T(8,128)(2,1)S(1)}, bf16[4,2,256,256]{3,2,1,0:T(8,128)(2,1)}, u32[]{:S(2)}) copy-start(bf16[4,2,256,256]{3,2,1,0:T(8,128)(2,1)} %constant.5.clone.tab_ref) | copy-start | bytes 3145732
  2.6 2.2 %copy-start.1 = (f32[16,256,256]{2,1,0:T(8,128)S(1)}, f32[16,256,256]{2,1,0:T(8,128)}, u32[]{:S(2)}) copy-start(f32[16,256,256]{2,1,0:T(8,128)} %meas_ref.1) | copy-start | bytes 12582916
  4.8 1.2 %copy-start.4 = (f32[2,256,512]{2,1,0:T(8,128)S(1)}, f32[2,256,512]{2,1,0:T(8,128)}, u32[]{:S(2)}) copy-start(f32[2,256,512]{2,1,0:T(8,128)} %obj_ref.1) | copy-start | bytes 3145732
  6.0 0.9 %copy-start.5 = (bf16[2,256,256]{2,1,0:T(8,128)(2,1)S(1)}, bf16[2,256,256]{2,1,0:T(8,128)(2,1)}, u32[]{:S(2)}) copy-start(bf16[2,256,256]{2,1,0:T(8,128)(2,1)} %constant.4.clone.perm_ref) | copy-start | bytes 786436
  23.5 1.9 %copy-start = (f32[16,256,256]{2,1,0:T(8,128)}, f32[16,256,256]{2,1,0:T(8,128)S(1)}, u32[]{:S(2)}) copy-start(f32[16,256,256]{2,1,0:T(8,128)S(1)} %get-tuple-element.7.meas_ref) | copy-start | bytes 12582916
  25.4 1.7 %copy-start.2 = (f32[2,6,512,128]{3,2,1,0:T(8,128)}, f32[2,6,512,128]{3,2,1,0:T(8,128)S(1)}, u32[]{:S(2)}) copy-start(f32[2,6,512,128]{3,2,1,0:T(8,128)S(1)} %get-tuple-element.6.ext_ref) | copy-start | bytes 9437188

commit v2 on v1

v2 whole, which is shorter than its diff:
```python
import functools
import math

import jax
import jax.numpy as jnp
import numpy as np
from jax import lax
from jax.experimental import pallas as pl
from jax.experimental.pallas import tpu as pltpu
from jax.sharding import PartitionSpec as P

LANES = 128
RIM = 128
F32 = jnp.float32
BF16 = jnp.bfloat16
MESH = pl.DeviceIdType.MESH


def dft_tables(size):
    half = size // 2
    n = np.arange(half)[:, None]
    k = np.arange(half)[None, :]
    out = []
    for parity in range(2):
        phase = (n * (2 * k + parity)) % size
        table = np.exp(-2j * np.pi * phase / size) / math.sqrt(size)
        real = np.block([[table.real, table.imag], [-table.imag, table.real]])
        out += [real, real.T]
    stack = np.stack(out)
    high = stack.astype(np.float32).astype(BF16)
    low = (stack - high.astype(np.float64)).astype(np.float32).astype(BF16)
    return np.stack([high, low], axis=1)


def split(value):
    high = value.astype(BF16)
    return high, (value - high.astype(F32)).astype(BF16)


def dot(a, b):
    return jnp.dot(a, b, preferred_element_type=F32)


def cat(parts, axis):
    return tuple(jnp.concatenate(p, axis=axis) for p in zip(*parts))


def one_position(chunk, row, col, meas, ext_ref, probe_ref, tab_ref, acc_ref, term_ref, rolled):
    size, half = 256, 128
    lane = lax.broadcasted_iota(jnp.int32, (chunk, LANES), 1)
    block = col // LANES
    shift = lax.rem(col, LANES)
    mask = lane >= shift

    def patch(start):
        rows = pl.ds(row + start, chunk)
        out = []
        for plane in range(2):
            b0 = ext_ref[plane, block, rows, :]
            b1 = ext_ref[plane, block + 1, rows, :]
            b2 = ext_ref[plane, block + 2, rows, :]
            out.append((jnp.where(mask, b0, b2), b1))
        return out

    sums, diffs = [], []
    for start in range(0, size, chunk):
        rows = pl.ds(start, chunk)
        (x0r, x1r), (x0i, x1i) = patch(start)
        pr = []
        for plane in range(2):
            r0 = pltpu.roll(probe_ref[plane, 0, rows, :], shift, 1)
            r1 = pltpu.roll(probe_ref[plane, 1, rows, :], shift, 1)
            p0 = jnp.where(mask, r0, r1)
            p1 = jnp.where(mask, r1, r0)
            rolled[plane, 0, rows, :] = p0
            rolled[plane, 1, rows, :] = p1
            pr.append((p0, p1))
        (p0r, p1r), (p0i, p1i) = pr
        e0r = p0r * x0r - p0i * x0i
        e0i = p0r * x0i + p0i * x0r
        e1r = p1r * x1r - p1i * x1i
        e1i = p1r * x1i + p1i * x1r
        sums.append(cat([split(e0r + e1r), split(e0i + e1i)], 1))
        diffs.append(cat([split(e0r - e1r), split(e0i - e1i)], 1))
    a, b = cat(sums, 0), cat(diffs, 0)

    def right(data, index):
        t = tab_ref[index, 0]
        return dot(data[0], t) + dot(data[1], t) + dot(data[0], tab_ref[index, 1])

    def left(index, data):
        t = tab_ref[index, 0]
        return dot(t, data[0]) + dot(t, data[1]) + dot(tab_ref[index, 1], data[0])

    yield
    ye = right(a, 0)
    yo = right(b, 2)
    yield
    s = [y[:half] + y[half:] for y in (ye, yo)]
    d = [y[:half] - y[half:] for y in (ye, yo)]
    a, b = [cat([cat([split(v[:, :LANES]) for v in w], 1), cat([split(v[:, LANES:]) for v in w], 1)], 0)
            for w in (s, d)]
    yield
    ze = left(1, a)
    zo = left(3, b)
    yield
    outs = []
    for z, first in ((ze, 0), (zo, half)):
        zr, zi = z[:half], z[half:]
        power = zr * zr + zi * zi
        factor = 1.0 - meas[pl.ds(first, half), :] * lax.rsqrt(jnp.maximum(power, 1.0))
        outs.append(cat([split(zr * factor), split(zi * factor)], 0))
    a, b = outs
    yield
    e = left(0, a)
    o = left(2, b)
    yield
    s, d = e + o, e - o
    a, b = [cat([cat([split(v[:half, cols]), split(v[half:, cols])], 1) for v in (s, d)], 0)
            for cols in (slice(0, LANES), slice(LANES, 2 * LANES))]
    yield
    e = right(a, 1)
    o = right(b, 3)
    yield
    back_shift = lax.rem(LANES - shift, LANES)
    keep = lane < LANES - shift
    for start in range(0, size, chunk):
        rows = pl.ds(start, chunk)
        ee, oo = e[start:start + chunk], o[start:start + chunk]
        b0, b1 = ee + oo, ee - oo
        b0r, b0i = b0[:, :LANES], b0[:, LANES:]
        b1r, b1i = b1[:, :LANES], b1[:, LANES:]
        p0r, p1r = rolled[0, 0, rows, :], rolled[0, 1, rows, :]
        p0i, p1i = rolled[1, 0, rows, :], rolled[1, 1, rows, :]
        grads = ((p0r * b0r + p0i * b0i, p1r * b1r + p1i * b1i),
                 (p0r * b0i - p0i * b0r, p1r * b1i - p1i * b1r))
        (x0r, x1r), (x0i, x1i) = patch(start)
        dst = pl.ds(row + start, chunk)
        for plane, (g0, g1) in enumerate(grads):
            acc_ref[plane, block, dst, :] += jnp.where(mask, g0, 0.0)
            acc_ref[plane, block + 1, dst, :] += g1
            acc_ref[plane, block + 2, dst, :] += jnp.where(mask, 0.0, g0)
        terms = ((x0r * b0r + x0i * b0i, x1r * b1r + x1i * b1i),
                 (x0r * b0i - x0i * b0r, x1r * b1i - x1i * b1r))
        for plane, (t0, t1) in enumerate(terms):
            r0 = pltpu.roll(t0, back_shift, 1)
            r1 = pltpu.roll(t1, back_shift, 1)
            term_ref[plane, 0, rows, :] += jnp.where(keep, r0, r1)
            term_ref[plane, 1, rows, :] += jnp.where(keep, r1, r0)


def compute_kernel(per_step, chunk, off_ref, ext_ref, probe_ref, meas_ref, tab_ref, acc_ref, term_ref, rolled):
    acc_ref[...] = jnp.zeros_like(acc_ref)
    term_ref[...] = jnp.zeros_like(term_ref)
    stages = 9

    def step(index, carry):
        live = []
        for slot in range(per_step):
            pos = index * per_step + slot
            row = lax.rem(off_ref[0, pos] + 128, 256)
            col = lax.rem(off_ref[1, pos] + 128, 512)
            live.append(one_position(chunk, row, col, meas_ref.at[pos], ext_ref, probe_ref, tab_ref,
                                     acc_ref, term_ref, rolled.at[slot]))
        for tick in range(stages + per_step - 1):
            for slot, gen in enumerate(live):
                if 0 <= tick - slot < stages:
                    next(gen, None)
        return carry

    lax.fori_loop(0, meas_ref.shape[0] // per_step, step, 0)


def compute(offsets, ext, probe, meas, tables, per_step=2, chunk=32):
    vmem = pl.BlockSpec(memory_space=pltpu.VMEM)
    return pl.pallas_call(
        functools.partial(compute_kernel, per_step, chunk),
        in_specs=[pl.BlockSpec(memory_space=pltpu.SMEM)] + [vmem] * 4,
        out_specs=[vmem] * 2,
        out_shape=[jax.ShapeDtypeStruct(ext.shape, F32), jax.ShapeDtypeStruct(probe.shape, F32)],
        scratch_shapes=[pltpu.VMEM((per_step, 2, 2, 256, 128), F32)],
        compiler_params=pltpu.CompilerParams(vmem_limit_bytes=32 * 2**20),
        name="updates",
    )(offsets, ext, probe, meas, tables)


POS, TILE = "pos", "tile"


def neighbour(dy, dx):
    p, t = lax.axis_index(POS), lax.axis_index(TILE)
    tp, tt = p + dx, t + dy
    inside = (tp >= 0) & (tp < lax.axis_size(POS)) & (tt >= 0) & (tt < lax.axis_size(TILE))
    return (tp, tt), inside


def greet(peers):
    barrier = pltpu.get_barrier_semaphore()
    for device, inside in peers:
        @pl.when(inside)
        def _():
            pl.semaphore_signal(barrier, inc=1, device_id=device, device_id_type=MESH)
    pl.semaphore_wait(barrier, sum(inside.astype(jnp.int32) for _, inside in peers))


def chip_side():
    core = lax.rem(lax.axis_index(TILE), 2)
    inner = 1 - 2 * core
    return core, inner, (lax.axis_index(POS), lax.axis_index(TILE) + inner)


def remote(src, dst, send, recv, device):
    return pltpu.make_async_remote_copy(src_ref=src, dst_ref=dst, send_sem=send, recv_sem=recv,
                                        device_id=device, device_id_type=MESH)


def when_each(condition, *calls):
    @pl.when(condition)
    def _():
        for call in calls:
            call()


def order_table(rows_first, size):
    out = lax.broadcasted_iota(jnp.int32, (size, size), 0 if rows_first else 1)
    src = lax.broadcasted_iota(jnp.int32, (size, size), 1 if rows_first else 0)
    half = size // 2
    wanted = jnp.where(out < half, 2 * out, 2 * out - size + 1)
    return jnp.where(src == wanted, 1.0, 0.0).astype(BF16)


def halo_kernel(obj_ref, meas_ref, prb_ref, ext_ref, out_ref, probe_ref, zeros, loaded, ordered, send_sem, recv_sem,
                fill_sem, own_sem, in_sem, out_sem, relay_send, relay_recv, probe_sem):
    group = loaded.shape[0] // in_sem.shape[0]
    size = loaded.shape[1]
    core, inner, partner = chip_side()
    p, t = lax.axis_index(POS), lax.axis_index(TILE)
    loads = [pltpu.make_async_copy(meas_ref.at[pl.ds(g * group, group)], loaded.at[pl.ds(g * group, group)], in_sem.at[g])
             for g in range(in_sem.shape[0])]
    locals_ = [pltpu.make_async_copy(obj_ref.at[:, :, pl.ds(b * LANES, LANES)], ext_ref.at[:, b + 1, pl.ds(RIM, 2 * RIM), :],
                                     own_sem.at[b]) for b in range(4)]
    locals_ += [pltpu.make_async_copy(prb_ref.at[:, :, pl.ds(b * LANES, LANES)], probe_ref.at[:, b], probe_sem.at[b])
                for b in range(2)]
    sides = [neighbour(0, -1), neighbour(0, 1)]
    outer, outer_in = neighbour(-inner, 0)
    corners = [neighbour(-inner, -1), neighbour(-inner, 1)]
    for load in loads:
        load.start()
    greet(sides + corners + [(outer, outer_in), (partner, p >= 0)])
    inner_row = pl.multiple_of((1 - core) * RIM, RIM)
    outer_row = pl.multiple_of(core * RIM, RIM)
    inner_halo = pl.multiple_of((1 - core) * 3 * RIM, RIM)
    outer_halo = pl.multiple_of(core * 3 * RIM, RIM)
    pairs = []

    def add(src_row, count, block, dst_block, dst_row, device, there, source_there, fill_row):
        index = len(pairs)
        copy = remote(obj_ref.at[:, pl.ds(src_row, count), pl.ds(block * LANES, LANES)],
                      ext_ref.at[:, dst_block, pl.ds(dst_row, count), :], send_sem.at[index], recv_sem.at[index], device)
        fill = pltpu.make_async_copy(zeros.at[:, pl.ds(0, count), :], ext_ref.at[:, dst_block, pl.ds(fill_row, count), :],
                                     fill_sem.at[index])
        pairs.append((copy, there, source_there, fill))
        when_each(there, copy.start)

    add(0, 2 * RIM, 0, 5, RIM, sides[0][0], sides[0][1], sides[1][1], RIM)
    add(0, 2 * RIM, 3, 0, RIM, sides[1][0], sides[1][1], sides[0][1], RIM)
    there_row = pl.multiple_of((1 - core) * 3 * RIM, RIM)
    for b in range(4):
        add(outer_row, RIM, b, b + 1, there_row, outer, outer_in, outer_in, outer_halo)
    add(outer_row, RIM, 0, 5, there_row, corners[0][0], corners[0][1], corners[1][1], outer_halo)
    add(outer_row, RIM, 3, 0, there_row, corners[1][0], corners[1][1], corners[0][1], outer_halo)
    partner_halo = pl.multiple_of(core * 3 * RIM, RIM)
    inside = [remote(obj_ref.at[:, pl.ds(inner_row, RIM), pl.ds(b * LANES, LANES)],
                     ext_ref.at[:, b + 1, pl.ds(partner_halo, RIM), :], relay_send.at[b], relay_recv.at[b], partner)
              for b in range(4)]
    for copy in inside:
        copy.start()
    for copy in locals_:
        copy.start()
    zeros[...] = jnp.zeros_like(zeros)
    for copy, there, source_there, fill in pairs:
        when_each(jnp.logical_not(source_there), fill.start)
    perm_rows, perm_cols = order_table(True, size), order_table(False, size)
    stores = []

    def relay():
        made = []
        inner_own = pl.multiple_of((2 - core) * RIM, RIM)
        for k, block in enumerate((5, 0)):
            copy, there, source_there, fill = pairs[k]
            when_each(source_there, copy.wait_recv)
            when_each(jnp.logical_not(source_there), fill.wait)
            here = ext_ref.at[:, block, pl.ds(inner_own, RIM), :]
            there_ref = ext_ref.at[:, block, pl.ds(partner_halo, RIM), :]
            made.append(remote(here, there_ref, relay_send.at[4 + k], relay_recv.at[4 + k], partner))
            made[-1].start()
        return made

    for g in range(in_sem.shape[0]):
        loads[g].wait()

        def order(i, carry):
            at = g * group + 2 * i
            parts = [split(loaded[at + j]) for j in range(2)]
            done = None
            for k in range(2):
                rows = jnp.concatenate([parts[0][k], parts[1][k]], axis=0)
                moved = dot(rows, perm_cols).astype(BF16)
                moved = jnp.concatenate([moved[:size], moved[size:]], axis=1)
                moved = dot(perm_rows, moved)
                done = moved if done is None else done + moved
            ordered[at] = done[:, :size]
            ordered[at + 1] = done[:, size:]
            return carry

        lax.fori_loop(0, group // 2, order, 0)
        store = pltpu.make_async_copy(ordered.at[pl.ds(g * group, group)], out_ref.at[pl.ds(g * group, group)], out_sem.at[g])
        store.start()
        stores.append(store)
    inside += relay()
    for copy in stores + locals_:
        copy.wait()
    for index, (copy, there, source_there, fill) in enumerate(pairs):
        when_each(there, copy.wait_send)
        if index >= 2:
            when_each(source_there, copy.wait_recv)
            when_each(jnp.logical_not(source_there), fill.wait)
    for copy in inside:
        copy.wait()


def exchange(object_field, measured, probe_field):
    groups = 4
    dma = pltpu.SemaphoreType.DMA
    anywhere = pl.BlockSpec(memory_space=pl.ANY)
    return pl.pallas_call(
        halo_kernel,
        in_specs=[pl.BlockSpec(memory_space=pltpu.HBM)] * 3,
        out_specs=[anywhere] * 3,
        out_shape=[jax.ShapeDtypeStruct((2, 6, 4 * RIM, LANES), F32), jax.ShapeDtypeStruct(measured.shape, F32),
                   jax.ShapeDtypeStruct((2, 2, 2 * RIM, LANES), F32)],
        scratch_shapes=[
            pltpu.VMEM((2, 2 * RIM, LANES), F32),
            pltpu.VMEM(measured.shape, F32),
            pltpu.VMEM(measured.shape, F32),
            dma((8,)), dma((8,)), dma((8,)),
            dma((4,)), dma((groups,)), dma((groups,)), dma((6,)), dma((6,)), dma((2,)),
        ],
        compiler_params=pltpu.CompilerParams(collective_id=0, has_side_effects=True, vmem_limit_bytes=16 * 2**20),
        name="halo",
    )(object_field, measured, probe_field)


LATE = 1
OUT_SPACE = pl.ANY


def gather_kernel(acc_ref, term_ref, obj_ref, probe_ref, own, total, result, *rest):
    (recv_v, recv_in, recv_c, recv_h, recv_d, side, part1, part2, part3,
     load_sem, send_sem, recv_sem, s1, r1, s2, r2, s3, r3, s4, r4, s5, r5, s6, r6, out_sem, pout_sem) = rest
    p, t = lax.axis_index(POS), lax.axis_index(TILE)
    x, z = p // 4, lax.rem(p, 4)
    y = t // 2
    core, inner, partner = chip_side()
    yz = y * 4 + z
    yes = p >= 0
    x_peers = [(lax.rem(x + k, 4) * 4 + z, t) for k in range(1, 4)]
    x_ids = [lax.rem(x + k, 4) for k in range(1, 4)]
    yz_ids = [lax.rem(yz + k, 16) for k in range(1, 16)]
    yz_peers = [(x * 4 + lax.rem(i, 4), (i // 4) * 2 + core) for i in yz_ids]
    sides = [neighbour(0, -1), neighbour(0, 1)]
    outer, outer_in = neighbour(-inner, 0)
    corners = [neighbour(-inner, -1), neighbour(-inner, 1)]

    load_total = pltpu.make_async_copy(term_ref, total, load_sem.at[0])
    load_own = pltpu.make_async_copy(acc_ref.at[:, pl.ds(1, 4), pl.ds(RIM, 2 * RIM), :], own, load_sem.at[1])
    load_sides = [pltpu.make_async_copy(acc_ref.at[:, b, pl.ds(RIM, 2 * RIM), :], side.at[k], load_sem.at[2 + k])
                  for k, b in enumerate((0, 5))]
    load_total.start()
    for load in load_sides:
        load.start()
    load_own.start()
    greet([(partner, yes), (outer, outer_in)] + sides + corners + [(d, yes) for d in x_peers] + [(d, yes) for d in yz_peers])
    load_total.wait()
    half = 512
    mine = pl.multiple_of(core * half, half)
    other = pl.multiple_of((1 - core) * half, half)
    first = remote(total.at[pl.ds(other, half)], part1, s1, r1, partner)
    first.start()
    inner_halo = pl.multiple_of((1 - core) * 3 * RIM, RIM)
    outer_halo = pl.multiple_of(core * 3 * RIM, RIM)
    count = 0

    def link(src, dst, device):
        nonlocal count
        copy = remote(src, dst, send_sem.at[count], recv_sem.at[count], device)
        count += 1
        return copy

    inner_corners = [link(acc_ref.at[:, b, pl.ds(inner_halo, RIM), :], recv_c.at[k], partner) for k, b in enumerate((0, 5))]
    for copy in inner_corners:
        copy.start()
    inner_main = link(acc_ref.at[:, pl.ds(1, 4), pl.ds(inner_halo, RIM), :], recv_in, partner)
    outer_main = link(acc_ref.at[:, pl.ds(1, 4), pl.ds(outer_halo, RIM), :], recv_v, outer)
    diagonal = [link(acc_ref.at[:, b, pl.ds(outer_halo, RIM), :], recv_d.at[k], corners[k][0]) for k, b in enumerate((0, 5))]
    across = [link(side.at[k], recv_h.at[k], sides[k][0]) for k in range(2)]
    when_each(outer_in, outer_main.start)
    for k in range(2):
        when_each(corners[k][1], diagonal[k].start)
    inner_main.start()
    first.wait()
    total[pl.ds(mine, half)] = total[pl.ds(mine, half)] + part1[...]
    quarter = half // 4
    seconds = [remote(total.at[pl.ds(pl.multiple_of(mine + i * quarter, quarter), quarter)], part2.at[k], s2.at[k], r2.at[k], d)
               for k, (i, d) in enumerate(zip(x_ids, x_peers))]
    for c in seconds:
        c.start()
    near = pl.multiple_of((1 - core) * RIM, RIM)
    for k in range(2):
        inner_corners[k].wait()
        load_sides[k].wait()
        side[k, :, pl.ds(near, RIM), :] = side[k, :, pl.ds(near, RIM), :] + recv_c[k]
        if not LATE:
            when_each(sides[k][1], across[k].start)
    at2 = pl.multiple_of(mine + x * quarter, quarter)
    for c in seconds:
        c.wait()
    total[pl.ds(at2, quarter)] = total[pl.ds(at2, quarter)] + part2[0] + part2[1] + part2[2]
    piece = quarter // 16
    thirds = [remote(total.at[pl.ds(pl.multiple_of(at2 + i * piece, piece), piece)], part3.at[k], s3.at[k], r3.at[k], d)
              for k, (i, d) in enumerate(zip(yz_ids, yz_peers))]
    for c in thirds:
        c.start()
    if LATE == 1:
        for k in range(2):
            when_each(sides[k][1], across[k].start)
    load_own.wait()
    far = pl.multiple_of(core * RIM, RIM)
    inner_main.wait()

    def add_rows(src, at):
        def body(i, carry):
            plane, b = i // 4, lax.rem(i, 4)
            own[plane, b, pl.ds(at, RIM), :] = own[plane, b, pl.ds(at, RIM), :] + src[plane, b]
            return carry
        lax.fori_loop(0, 8, body, 0)

    add_rows(recv_in, near)
    for c in thirds:
        c.wait()
    at3 = pl.multiple_of(at2 + yz * piece, piece)
    value = total[pl.ds(at3, piece)]
    for k in range(15):
        value = value + part3[k]
    result[pl.ds(at3, piece)] = value * (1.0 / math.sqrt(2048))
    here = result.at[pl.ds(at3, piece)]
    fourths = [remote(here, here, s4.at[k], r4.at[k], d) for k, d in enumerate(yz_peers)]
    for c in fourths:
        c.start()
    if LATE == 2:
        for k in range(2):
            when_each(sides[k][1], across[k].start)

    @pl.when(outer_in)
    def _():
        outer_main.wait()
        add_rows(recv_v, far)

    outs = [pltpu.make_async_copy(own.at[:, b], obj_ref.at[:, :, pl.ds(b * LANES, LANES)], out_sem.at[b]) for b in range(4)]
    for b in (1, 2):
        outs[b].start()
    for c in fourths:
        c.wait()
    here2 = result.at[pl.ds(at2, quarter)]
    fifths = [remote(here2, here2, s5.at[k], r5.at[k], d) for k, d in enumerate(x_peers)]
    for c in fifths:
        c.start()
    for k in range(2):
        block = 3 - 3 * k
        source, diagonal_source = sides[1 - k][1], corners[1 - k][1]

        @pl.when(source)
        def _():
            across[k].wait_recv()
            own[:, block] = own[:, block] + recv_h[k]

        @pl.when(diagonal_source)
        def _():
            diagonal[k].wait_recv()
            own[:, block, pl.ds(far, RIM), :] = own[:, block, pl.ds(far, RIM), :] + recv_d[k]

        outs[block].start()
    for c in fifths:
        c.wait()
    here1 = result.at[pl.ds(mine, half)]
    last = remote(here1, here1, s6, r6, partner)
    last.start()
    for k in range(2):
        when_each(sides[k][1], across[k].wait_send)
        when_each(corners[k][1], diagonal[k].wait_send)
    last.wait()
    for i in range(4):
        out = pltpu.make_async_copy(result.at[pl.ds(i * 256, 256)], probe_ref.at[i // 2, :, pl.ds((i % 2) * LANES, LANES)], pout_sem.at[i])
        out.start()
        outs.append(out)
    for out in outs:
        out.wait()


def collect(acc, term):
    dma = pltpu.SemaphoreType.DMA
    vmem = lambda *shape: pltpu.VMEM(shape, F32)
    return pl.pallas_call(
        gather_kernel,
        in_specs=[pl.BlockSpec(memory_space=pl.ANY)] * 2,
        out_specs=[pl.BlockSpec(memory_space=OUT_SPACE)] * 2,
        out_shape=[jax.ShapeDtypeStruct((2, 256, 512), F32), jax.ShapeDtypeStruct((2, 256, 256), F32)],
        scratch_shapes=[
            vmem(2, 4, 2 * RIM, LANES), vmem(1024, LANES), vmem(1024, LANES),
            vmem(2, 4, RIM, LANES), vmem(2, 4, RIM, LANES), vmem(2, 2, RIM, LANES), vmem(2, 2, 2 * RIM, LANES),
            vmem(2, 2, RIM, LANES), vmem(2, 2, 2 * RIM, LANES),
            vmem(512, LANES), vmem(3, 128, LANES), vmem(15, 8, LANES),
            dma((4,)), dma((8,)), dma((8,)), dma, dma, dma((3,)), dma((3,)), dma((15,)), dma((15,)),
            dma((15,)), dma((15,)), dma((3,)), dma((3,)), dma, dma, dma((4,)), dma((4,)),
        ],
        compiler_params=pltpu.CompilerParams(collective_id=1, has_side_effects=True, vmem_limit_bytes=16 * 2**20),
        name="collect",
    )(acc, term.reshape(1024, LANES))


def on_device(object_field, probe_field, measured, offsets):
    fixed = [pltpu.with_memory_space_constraint(a, pltpu.HBM) for a in (object_field, measured, probe_field)]
    ext, ordered, probe = exchange(*fixed)
    acc, term = compute(offsets.T, ext, probe, ordered, jnp.asarray(dft_tables(256)))
    return collect(acc, term)


def solution(mesh):
    placed = (P(None, "tile", "pos"), P(), P(("pos", "tile"), None, None), P(("pos", "tile"), None))
    return jax.shard_map(
        on_device,
        mesh=mesh,
        in_specs=placed,
        out_specs=(P(None, "tile", "pos"), P()),
        check_vma=False,
    )
```

time: 94.6 us -> 74 us (0.78)
  Pallas kernels: 82 us -> 71.4 us
  local copies, waits for them, and re-layouts: 11.6 us -> 1.78 us
    unnamed x15 -> x6, local copies, waits for them, and re-layouts: 10.6 us -> 1.78 us
    pallas_call x1, Pallas kernels: 43 us -> 34.8 us  [collect(): pl.pallas_call(gather_kernel, in_specs=[pl.BlockSpec(memory_space=pl.ANY)...]
    pallas_call x2, Pallas kernels: 38.9 us -> 36.6 us  [the longest x1 21.5 us: compute(): pl.pallas_call(functools.partial(compute_kernel, per_step, chunk), in_spe...]
    another operation x1 -> x0, local copies, waits for them, and re-layouts: 1.06 us -> none  [on_device(): jnp.stack([probe_field[:, :, :LANES], probe_field[:, :, LANES:]], axis=1)]
where the time goes in v2:
time: 74 us; the launch traced here: 73.9 us
  Pallas kernels  71.4 us (96%)
  local copies, waits for them, and re-layouts  1.78 us (2%)
    pallas_call x1, Pallas kernels, collect(): pl.pallas_call(gather_kernel, in_specs=[pl.BlockSpec(memory_space=pl.ANY)...  34.8 us
    pallas_call x1, Pallas kernels, compute(): pl.pallas_call(functools.partial(compute_kernel, per_step, chunk), in_spe...  21.5 us
    pallas_call x1, Pallas kernels, exchange(): pl.pallas_call(halo_kernel, in_specs=[pl.BlockSpec(memory_space=pltpu.HBM...  15 us
    unnamed x6, local copies, waits for them, and re-layouts  1.78 us

profile of v2, /device:TPU:1, one launch (start us, length us, event | category | flops | bytes accessed | tf_op | source)
XLA Modules:
  0.0 73.9 jit_solution(2339053308050886646)
XLA Ops:
  0.6 0.0 copy-start
  0.6 0.0 copy-start.1
  0.7 15.0 %halo.1 = (f32[2,6,512,128]{3,2,1,0:T(8,128)S(1)}, f32[16,256,256]{2,1,0:T(8,128)S(1)}, f32[2,2,256,128]{3,2,1,0:T(8,128)S(1)}) custom-call(f32[2,256,512]{2,1,0:T(8,128)} %obj_ref.1, f32[16,256,256]{2,1,0:T(8,128)} %meas_ref.1, f32[2,256,256]{2,1,0:T(8,128)} %prb_ref.1), custom_call_target="tpu_custom_call" | custom-call | tf_op jit(solution)/shard_map/halo/pallas_call | solution.py:336
  15.7 0.0 copy-done
  15.7 0.0 copy-done.1
  15.7 21.5 %updates.1 = (f32[2,6,512,128]{3,2,1,0:T(8,128)S(1)}, f32[2,2,256,128]{3,2,1,0:T(8,128)S(1)}) custom-call(s32[2,16]{1,0:T(2,128)S(1)} %bitcast.3, f32[2,6,512,128]{3,2,1,0:T(8,128)S(1)} %get-tuple-element.7.ext_ref, f32[2,2,256,128]{3,2,1,0:T(8,128)S(1)} %get-tuple-element.8.probe_ref, f32[16,256,256]{2,1,0:T(8,128)S(1)} %get-tuple-element.9.meas_ref, ...), custom_call_target="tpu_custom_call" | custom-call | tf_op jit(solution)/shard_map/updates/pallas_call | solution.py:176
  37.2 34.8 %collect.1 = (f32[2,256,512]{2,1,0:T(8,128)S(1)}, f32[2,256,256]{2,1,0:T(8,128)S(1)}) custom-call(f32[2,6,512,128]{3,2,1,0:T(8,128)S(1)} %get-tuple-element.10.acc_ref, f32[1024,128]{1,0:T(8,128)S(1)} %bitcast.2), custom_call_target="tpu_custom_call" | custom-call | tf_op jit(solution)/shard_map/collect/pallas_call | solution.py:513
  72.1 1.0 %copy.9 = f32[2,256,512]{2,1,0:T(8,128)} copy(f32[2,256,512]{2,1,0:T(8,128)S(1)} %get-tuple-element.14) | data formatting | bytes 2097152
  73.1 0.8 %copy.10 = f32[2,256,256]{2,1,0:T(8,128)} copy(f32[2,256,256]{2,1,0:T(8,128)S(1)} %get-tuple-element.15) | data formatting | bytes 1048576
Async XLA Ops:
  0.6 15.1 %copy-start = (bf16[4,2,256,256]{3,2,1,0:T(8,128)(2,1)S(1)}, bf16[4,2,256,256]{3,2,1,0:T(8,128)(2,1)}, u32[]{:S(2)}) copy-start(bf16[4,2,256,256]{3,2,1,0:T(8,128)(2,1)} %constant.2.clone.tab_ref) | copy-start | bytes 3145732
  0.6 15.1 %copy-start.1 = (s32[16,2]{0,1:T(2,128)S(1)}, s32[16,2]{0,1:T(2,128)}, u32[]{:S(2)}) copy-start(s32[16,2]{0,1:T(2,128)} %param.8) | copy-start | bytes 388

commit v3 on v2

--- a/solution.py
+++ b/solution.py
@@ -171,7 +171,7 @@
     lax.fori_loop(0, meas_ref.shape[0] // per_step, step, 0)
 
 
-def compute(offsets, ext, probe, meas, tables, per_step=2, chunk=32):
+def compute(offsets, ext, probe, meas, tables, per_step=4, chunk=32):
     vmem = pl.BlockSpec(memory_space=pltpu.VMEM)
     return pl.pallas_call(
         functools.partial(compute_kernel, per_step, chunk),
@@ -351,10 +351,6 @@
     )(object_field, measured, probe_field)
 
 
-LATE = 1
-OUT_SPACE = pl.ANY
-
-
 def gather_kernel(acc_ref, term_ref, obj_ref, probe_ref, own, total, result, *rest):
     (recv_v, recv_in, recv_c, recv_h, recv_d, side, part1, part2, part3,
      load_sem, send_sem, recv_sem, s1, r1, s2, r2, s3, r3, s4, r4, s5, r5, s6, r6, out_sem, pout_sem) = rest
@@ -385,8 +381,12 @@
     half = 512
     mine = pl.multiple_of(core * half, half)
     other = pl.multiple_of((1 - core) * half, half)
-    first = remote(total.at[pl.ds(other, half)], part1, s1, r1, partner)
-    first.start()
+    quarter = half // 4
+    order = x_ids + [x]
+    firsts = [remote(total.at[pl.ds(pl.multiple_of(other + i * quarter, quarter), quarter)], part1.at[k], s1.at[k], r1.at[k], partner)
+              for k, i in enumerate(order)]
+    for c in firsts:
+        c.start()
     inner_halo = pl.multiple_of((1 - core) * 3 * RIM, RIM)
     outer_halo = pl.multiple_of(core * 3 * RIM, RIM)
     count = 0
@@ -405,35 +405,30 @@
     diagonal = [link(acc_ref.at[:, b, pl.ds(outer_halo, RIM), :], recv_d.at[k], corners[k][0]) for k, b in enumerate((0, 5))]
     across = [link(side.at[k], recv_h.at[k], sides[k][0]) for k in range(2)]
     when_each(outer_in, outer_main.start)
-    for k in range(2):
-        when_each(corners[k][1], diagonal[k].start)
+    seconds = []
+    for k, i in enumerate(order):
+        firsts[k].wait_recv()
+        rows = pl.ds(pl.multiple_of(mine + i * quarter, quarter), quarter)
+        total[rows] = total[rows] + part1[k]
+        if k < 3:
+            seconds.append(remote(total.at[rows], part2.at[k], s2.at[k], r2.at[k], x_peers[k]))
+            seconds[k].start()
     inner_main.start()
-    first.wait()
-    total[pl.ds(mine, half)] = total[pl.ds(mine, half)] + part1[...]
-    quarter = half // 4
-    seconds = [remote(total.at[pl.ds(pl.multiple_of(mine + i * quarter, quarter), quarter)], part2.at[k], s2.at[k], r2.at[k], d)
-               for k, (i, d) in enumerate(zip(x_ids, x_peers))]
-    for c in seconds:
-        c.start()
     near = pl.multiple_of((1 - core) * RIM, RIM)
     for k in range(2):
         inner_corners[k].wait()
         load_sides[k].wait()
         side[k, :, pl.ds(near, RIM), :] = side[k, :, pl.ds(near, RIM), :] + recv_c[k]
-        if not LATE:
-            when_each(sides[k][1], across[k].start)
+        when_each(sides[k][1], across[k].start)
     at2 = pl.multiple_of(mine + x * quarter, quarter)
     for c in seconds:
-        c.wait()
+        c.wait_recv()
     total[pl.ds(at2, quarter)] = total[pl.ds(at2, quarter)] + part2[0] + part2[1] + part2[2]
     piece = quarter // 16
     thirds = [remote(total.at[pl.ds(pl.multiple_of(at2 + i * piece, piece), piece)], part3.at[k], s3.at[k], r3.at[k], d)
               for k, (i, d) in enumerate(zip(yz_ids, yz_peers))]
     for c in thirds:
         c.start()
-    if LATE == 1:
-        for k in range(2):
-            when_each(sides[k][1], across[k].start)
     load_own.wait()
     far = pl.multiple_of(core * RIM, RIM)
     inner_main.wait()
@@ -447,7 +442,7 @@
 
     add_rows(recv_in, near)
     for c in thirds:
-        c.wait()
+        c.wait_recv()
     at3 = pl.multiple_of(at2 + yz * piece, piece)
     value = total[pl.ds(at3, piece)]
     for k in range(15):
@@ -457,9 +452,6 @@
     fourths = [remote(here, here, s4.at[k], r4.at[k], d) for k, d in enumerate(yz_peers)]
     for c in fourths:
         c.start()
-    if LATE == 2:
-        for k in range(2):
-            when_each(sides[k][1], across[k].start)
 
     @pl.when(outer_in)
     def _():
@@ -470,11 +462,15 @@
     for b in (1, 2):
         outs[b].start()
     for c in fourths:
-        c.wait()
+        c.wait_recv()
     here2 = result.at[pl.ds(at2, quarter)]
     fifths = [remote(here2, here2, s5.at[k], r5.at[k], d) for k, d in enumerate(x_peers)]
     for c in fifths:
         c.start()
+    lasts = [remote(here2, here2, s6.at[3], r6.at[3], partner)]
+    lasts[0].start()
+    for k in range(2):
+        when_each(corners[k][1], diagonal[k].start)
     for k in range(2):
         block = 3 - 3 * k
         source, diagonal_source = sides[1 - k][1], corners[1 - k][1]
@@ -490,19 +486,25 @@
             own[:, block, pl.ds(far, RIM), :] = own[:, block, pl.ds(far, RIM), :] + recv_d[k]
 
         outs[block].start()
-    for c in fifths:
-        c.wait()
-    here1 = result.at[pl.ds(mine, half)]
-    last = remote(here1, here1, s6, r6, partner)
-    last.start()
+    for k, c in enumerate(fifths):
+        c.wait_recv()
+        from_x = lax.rem(x + 3 - k, 4)
+        here1 = result.at[pl.ds(pl.multiple_of(mine + from_x * quarter, quarter), quarter)]
+        lasts.append(remote(here1, here1, s6.at[k], r6.at[k], partner))
+        lasts[-1].start()
+    for plane, ready in ((core, ()), (1 - core, lasts)):
+        for c in ready:
+            c.wait_recv()
+        for b in range(2):
+            rows = pl.ds(pl.multiple_of(plane * half + b * (half // 2), half // 2), half // 2)
+            out = pltpu.make_async_copy(result.at[rows], probe_ref.at[plane, :, pl.ds(b * LANES, LANES)], pout_sem.at[len(outs) - 4])
+            out.start()
+            outs.append(out)
+    for c in firsts + seconds + thirds + fourths + fifths + lasts:
+        c.wait_send()
     for k in range(2):
         when_each(sides[k][1], across[k].wait_send)
         when_each(corners[k][1], diagonal[k].wait_send)
-    last.wait()
-    for i in range(4):
-        out = pltpu.make_async_copy(result.at[pl.ds(i * 256, 256)], probe_ref.at[i // 2, :, pl.ds((i % 2) * LANES, LANES)], pout_sem.at[i])
-        out.start()
-        outs.append(out)
     for out in outs:
         out.wait()
 
@@ -513,15 +515,15 @@
     return pl.pallas_call(
         gather_kernel,
         in_specs=[pl.BlockSpec(memory_space=pl.ANY)] * 2,
-        out_specs=[pl.BlockSpec(memory_space=OUT_SPACE)] * 2,
+        out_specs=[pl.BlockSpec(memory_space=pl.ANY)] * 2,
         out_shape=[jax.ShapeDtypeStruct((2, 256, 512), F32), jax.ShapeDtypeStruct((2, 256, 256), F32)],
         scratch_shapes=[
             vmem(2, 4, 2 * RIM, LANES), vmem(1024, LANES), vmem(1024, LANES),
             vmem(2, 4, RIM, LANES), vmem(2, 4, RIM, LANES), vmem(2, 2, RIM, LANES), vmem(2, 2, 2 * RIM, LANES),
             vmem(2, 2, RIM, LANES), vmem(2, 2, 2 * RIM, LANES),
-            vmem(512, LANES), vmem(3, 128, LANES), vmem(15, 8, LANES),
-            dma((4,)), dma((8,)), dma((8,)), dma, dma, dma((3,)), dma((3,)), dma((15,)), dma((15,)),
-            dma((15,)), dma((15,)), dma((3,)), dma((3,)), dma, dma, dma((4,)), dma((4,)),
+            vmem(4, 128, LANES), vmem(3, 128, LANES), vmem(15, 8, LANES),
+            dma((4,)), dma((8,)), dma((8,)), dma((4,)), dma((4,)), dma((3,)), dma((3,)), dma((15,)), dma((15,)),
+            dma((15,)), dma((15,)), dma((3,)), dma((3,)), dma((4,)), dma((4,)), dma((4,)), dma((4,)),
         ],
         compiler_params=pltpu.CompilerParams(collective_id=1, has_side_effects=True, vmem_limit_bytes=16 * 2**20),
         name="collect",

time: 74 us -> 71.1 us (0.961)
  Pallas kernels: 71.4 us -> 68.2 us
    pallas_call x1, Pallas kernels: 34.8 us -> 32.3 us  [collect(): pl.pallas_call(gather_kernel, in_specs=[pl.BlockSpec(memory_space=pl.ANY)...]
where the time goes in v3:
time: 71.1 us; the launch traced here: 70.7 us
  Pallas kernels  68.2 us (96%)
  local copies, waits for them, and re-layouts  1.78 us (3%)
    pallas_call x1, Pallas kernels, collect(): pl.pallas_call(gather_kernel, in_specs=[pl.BlockSpec(memory_space=pl.ANY)...  32.3 us
    pallas_call x1, Pallas kernels, compute(): pl.pallas_call(functools.partial(compute_kernel, per_step, chunk), in_spe...  20.9 us
    pallas_call x1, Pallas kernels, exchange(): pl.pallas_call(halo_kernel, in_specs=[pl.BlockSpec(memory_space=pltpu.HBM...  15 us
    unnamed x6, local copies, waits for them, and re-layouts  1.78 us

profile of v3, /device:TPU:1, one launch (start us, length us, event | category | flops | bytes accessed | tf_op | source)
XLA Modules:
  0.0 70.7 jit_solution(9412776419520030032)
XLA Ops:
  0.6 0.0 copy-start
  0.6 0.0 copy-start.1
  0.7 15.0 %halo.1 = (f32[2,6,512,128]{3,2,1,0:T(8,128)S(1)}, f32[16,256,256]{2,1,0:T(8,128)S(1)}, f32[2,2,256,128]{3,2,1,0:T(8,128)S(1)}) custom-call(f32[2,256,512]{2,1,0:T(8,128)} %obj_ref.1, f32[16,256,256]{2,1,0:T(8,128)} %meas_ref.1, f32[2,256,256]{2,1,0:T(8,128)} %prb_ref.1), custom_call_target="tpu_custom_call" | custom-call | tf_op jit(solution)/shard_map/halo/pallas_call | solution.py:336
  15.7 0.0 copy-done
  15.7 0.0 copy-done.1
  15.7 20.9 %updates.1 = (f32[2,6,512,128]{3,2,1,0:T(8,128)S(1)}, f32[2,2,256,128]{3,2,1,0:T(8,128)S(1)}) custom-call(s32[2,16]{1,0:T(2,128)S(1)} %bitcast.3, f32[2,6,512,128]{3,2,1,0:T(8,128)S(1)} %get-tuple-element.7.ext_ref, f32[2,2,256,128]{3,2,1,0:T(8,128)S(1)} %get-tuple-element.8.probe_ref, f32[16,256,256]{2,1,0:T(8,128)S(1)} %get-tuple-element.9.meas_ref, ...), custom_call_target="tpu_custom_call" | custom-call | tf_op jit(solution)/shard_map/updates/pallas_call | solution.py:176
  36.7 32.3 %collect.1 = (f32[2,256,512]{2,1,0:T(8,128)S(1)}, f32[2,256,256]{2,1,0:T(8,128)S(1)}) custom-call(f32[2,6,512,128]{3,2,1,0:T(8,128)S(1)} %get-tuple-element.10.acc_ref, f32[1024,128]{1,0:T(8,128)S(1)} %bitcast.2), custom_call_target="tpu_custom_call" | custom-call | tf_op jit(solution)/shard_map/collect/pallas_call | solution.py:515
  68.9 1.0 %copy.9 = f32[2,256,512]{2,1,0:T(8,128)} copy(f32[2,256,512]{2,1,0:T(8,128)S(1)} %get-tuple-element.14) | data formatting | bytes 2097152
  69.9 0.8 %copy.10 = f32[2,256,256]{2,1,0:T(8,128)} copy(f32[2,256,256]{2,1,0:T(8,128)S(1)} %get-tuple-element.15) | data formatting | bytes 1048576
Async XLA Ops:
  0.6 15.1 %copy-start = (bf16[4,2,256,256]{3,2,1,0:T(8,128)(2,1)S(1)}, bf16[4,2,256,256]{3,2,1,0:T(8,128)(2,1)}, u32[]{:S(2)}) copy-start(bf16[4,2,256,256]{3,2,1,0:T(8,128)(2,1)} %constant.2.clone.tab_ref) | copy-start | bytes 3145732
  0.6 15.1 %copy-start.1 = (s32[16,2]{0,1:T(2,128)S(1)}, s32[16,2]{0,1:T(2,128)}, u32[]{:S(2)}) copy-start(s32[16,2]{0,1:T(2,128)} %param.8) | copy-start | bytes 388

commit v4 on v3

--- a/solution.py
+++ b/solution.py
@@ -32,6 +32,23 @@
     return np.stack([high, low], axis=1)
 
 
+def row_tables(size):
+    quarter = size // 4
+    n = np.arange(quarter)[:, None]
+    k = np.arange(quarter)[None, :]
+    out = []
+    for residue in range(4):
+        phase = (n * (4 * k + residue)) % size
+        table = np.exp(-2j * np.pi * phase / size) / math.sqrt(size)
+        real = np.block([[table.real, table.imag], [-table.imag, table.real]])
+        out.append([real.T, real])
+    stack = np.array(out).transpose(1, 0, 2, 3)
+    high = stack.astype(np.float32).astype(BF16)
+    low = (stack - high.astype(np.float64)).astype(np.float32).astype(BF16)
+    both = np.concatenate([high, high], axis=-1)
+    return np.concatenate([both, np.concatenate([low, np.zeros_like(low)], axis=-1)], axis=2)
+
+
 def split(value):
     high = value.astype(BF16)
     return high, (value - high.astype(F32)).astype(BF16)
@@ -45,7 +62,7 @@
     return tuple(jnp.concatenate(p, axis=axis) for p in zip(*parts))
 
 
-def one_position(chunk, row, col, meas, ext_ref, probe_ref, tab_ref, acc_ref, term_ref, rolled):
+def one_position(chunk, row, col, meas, ext_ref, probe_ref, tab_ref, rtab_ref, acc_ref, term_ref, rolled):
     size, half = 256, 128
     lane = lax.broadcasted_iota(jnp.int32, (chunk, LANES), 1)
     block = col // LANES
@@ -88,35 +105,47 @@
         t = tab_ref[index, 0]
         return dot(data[0], t) + dot(data[1], t) + dot(data[0], tab_ref[index, 1])
 
-    def left(index, data):
-        t = tab_ref[index, 0]
-        return dot(t, data[0]) + dot(t, data[1]) + dot(tab_ref[index, 1], data[0])
+    def left(inverse, residue, stacked):
+        product = dot(rtab_ref[inverse, residue], stacked)
+        return product[:size // 2] + product[size // 2:]
+
+    def stack(real, imag):
+        (rh, rl), (ih, il) = split(real), split(imag)
+        return jnp.concatenate([rh, ih, rl, il], axis=0)
 
     yield
     ye = right(a, 0)
     yo = right(b, 2)
     yield
-    s = [y[:half] + y[half:] for y in (ye, yo)]
-    d = [y[:half] - y[half:] for y in (ye, yo)]
-    a, b = [cat([cat([split(v[:, :LANES]) for v in w], 1), cat([split(v[:, LANES:]) for v in w], 1)], 0)
-            for w in (s, d)]
-    yield
-    ze = left(1, a)
-    zo = left(3, b)
-    yield
-    outs = []
-    for z, first in ((ze, 0), (zo, half)):
-        zr, zi = z[:half], z[half:]
+    quarter = size // 4
+
+    def both(part, m):
+        rows = slice(m * quarter, (m + 1) * quarter)
+        cols = slice(part * LANES, (part + 1) * LANES)
+        return jnp.concatenate([ye[rows, cols], yo[rows, cols]], axis=1)
+
+    re, im = [[both(part, m) for m in range(4)] for part in range(2)]
+    t0, t1, t2, t3 = [(re[0] + re[2], im[0] + im[2]), (re[0] - re[2], im[0] - im[2]),
+                      (re[1] + re[3], im[1] + im[3]), (re[1] - re[3], im[1] - im[3])]
+    inputs = [stack(t0[0] + t2[0], t0[1] + t2[1]), stack(t1[0] + t3[1], t1[1] - t3[0]),
+              stack(t0[0] - t2[0], t0[1] - t2[1]), stack(t1[0] - t3[1], t1[1] + t3[0])]
+    yield
+    waves = [left(0, q, inputs[q]) for q in range(4)]
+    yield
+    inputs = []
+    for q, z in enumerate(waves):
+        zr, zi = z[:quarter], z[quarter:]
         power = zr * zr + zi * zi
-        factor = 1.0 - meas[pl.ds(first, half), :] * lax.rsqrt(jnp.maximum(power, 1.0))
-        outs.append(cat([split(zr * factor), split(zi * factor)], 0))
-    a, b = outs
-    yield
-    e = left(0, a)
-    o = left(2, b)
-    yield
-    s, d = e + o, e - o
-    a, b = [cat([cat([split(v[:half, cols]), split(v[half:, cols])], 1) for v in (s, d)], 0)
+        factor = 1.0 - meas[pl.ds(q * quarter, quarter), :] * lax.rsqrt(jnp.maximum(power, 1.0))
+        inputs.append(stack(zr * factor, zi * factor))
+    yield
+    v = [left(1, q, inputs[q]) for q in range(4)]
+    v = [(w[:quarter], w[quarter:]) for w in v]
+    yield
+    (s0r, s1r, s2r, s3r), (s0i, s1i, s2i, s3i) = [
+        (v[0][c] + v[2][c], v[0][c] - v[2][c], v[1][c] + v[3][c], v[1][c] - v[3][c]) for c in range(2)]
+    outs = [(s0r + s2r, s0i + s2i), (s1r - s3i, s1i + s3r), (s0r - s2r, s0i - s2i), (s1r + s3i, s1i - s3r)]
+    a, b = [cat([cat([split(xr[:, cols]), split(xi[:, cols])], 1) for xr, xi in outs], 0)
             for cols in (slice(0, LANES), slice(LANES, 2 * LANES))]
     yield
     e = right(a, 1)
@@ -149,7 +178,7 @@
             term_ref[plane, 1, rows, :] += jnp.where(keep, r1, r0)
 
 
-def compute_kernel(per_step, chunk, off_ref, ext_ref, probe_ref, meas_ref, tab_ref, acc_ref, term_ref, rolled):
+def compute_kernel(per_step, chunk, off_ref, ext_ref, probe_ref, meas_ref, tab_ref, rtab_ref, acc_ref, term_ref, rolled):
     acc_ref[...] = jnp.zeros_like(acc_ref)
     term_ref[...] = jnp.zeros_like(term_ref)
     stages = 9
@@ -160,7 +189,7 @@
             pos = index * per_step + slot
             row = lax.rem(off_ref[0, pos] + 128, 256)
             col = lax.rem(off_ref[1, pos] + 128, 512)
-            live.append(one_position(chunk, row, col, meas_ref.at[pos], ext_ref, probe_ref, tab_ref,
+            live.append(one_position(chunk, row, col, meas_ref.at[pos], ext_ref, probe_ref, tab_ref, rtab_ref,
                                      acc_ref, term_ref, rolled.at[slot]))
         for tick in range(stages + per_step - 1):
             for slot, gen in enumerate(live):
@@ -171,17 +200,17 @@
     lax.fori_loop(0, meas_ref.shape[0] // per_step, step, 0)
 
 
-def compute(offsets, ext, probe, meas, tables, per_step=4, chunk=32):
+def compute(offsets, ext, probe, meas, tables, rows, per_step=4, chunk=32):
     vmem = pl.BlockSpec(memory_space=pltpu.VMEM)
     return pl.pallas_call(
         functools.partial(compute_kernel, per_step, chunk),
-        in_specs=[pl.BlockSpec(memory_space=pltpu.SMEM)] + [vmem] * 4,
+        in_specs=[pl.BlockSpec(memory_space=pltpu.SMEM)] + [vmem] * 5,
         out_specs=[vmem] * 2,
         out_shape=[jax.ShapeDtypeStruct(ext.shape, F32), jax.ShapeDtypeStruct(probe.shape, F32)],
         scratch_shapes=[pltpu.VMEM((per_step, 2, 2, 256, 128), F32)],
         compiler_params=pltpu.CompilerParams(vmem_limit_bytes=32 * 2**20),
         name="updates",
-    )(offsets, ext, probe, meas, tables)
+    )(offsets, ext, probe, meas, tables, rows)
 
 
 POS, TILE = "pos", "tile"
@@ -224,8 +253,8 @@
 def order_table(rows_first, size):
     out = lax.broadcasted_iota(jnp.int32, (size, size), 0 if rows_first else 1)
     src = lax.broadcasted_iota(jnp.int32, (size, size), 1 if rows_first else 0)
-    half = size // 2
-    wanted = jnp.where(out < half, 2 * out, 2 * out - size + 1)
+    radix = 4 if rows_first else 2
+    wanted = lax.rem(out, size // radix) * radix + out // (size // radix)
     return jnp.where(src == wanted, 1.0, 0.0).astype(BF16)
 
 
@@ -351,9 +380,9 @@
     )(object_field, measured, probe_field)
 
 
-def gather_kernel(acc_ref, term_ref, obj_ref, probe_ref, own, total, result, *rest):
+def gather_kernel(acc_ref, term_ref, own, result, total, *rest):
     (recv_v, recv_in, recv_c, recv_h, recv_d, side, part1, part2, part3,
-     load_sem, send_sem, recv_sem, s1, r1, s2, r2, s3, r3, s4, r4, s5, r5, s6, r6, out_sem, pout_sem) = rest
+     load_sem, send_sem, recv_sem, s1, r1, s2, r2, s3, r3, s4, r4, s5, r5, s6, r6) = rest
     p, t = lax.axis_index(POS), lax.axis_index(TILE)
     x, z = p // 4, lax.rem(p, 4)
     y = t // 2
@@ -458,9 +487,6 @@
         outer_main.wait()
         add_rows(recv_v, far)
 
-    outs = [pltpu.make_async_copy(own.at[:, b], obj_ref.at[:, :, pl.ds(b * LANES, LANES)], out_sem.at[b]) for b in range(4)]
-    for b in (1, 2):
-        outs[b].start()
     for c in fourths:
         c.wait_recv()
     here2 = result.at[pl.ds(at2, quarter)]
@@ -484,29 +510,19 @@
         def _():
             diagonal[k].wait_recv()
             own[:, block, pl.ds(far, RIM), :] = own[:, block, pl.ds(far, RIM), :] + recv_d[k]
-
-        outs[block].start()
     for k, c in enumerate(fifths):
         c.wait_recv()
         from_x = lax.rem(x + 3 - k, 4)
         here1 = result.at[pl.ds(pl.multiple_of(mine + from_x * quarter, quarter), quarter)]
         lasts.append(remote(here1, here1, s6.at[k], r6.at[k], partner))
         lasts[-1].start()
-    for plane, ready in ((core, ()), (1 - core, lasts)):
-        for c in ready:
-            c.wait_recv()
-        for b in range(2):
-            rows = pl.ds(pl.multiple_of(plane * half + b * (half // 2), half // 2), half // 2)
-            out = pltpu.make_async_copy(result.at[rows], probe_ref.at[plane, :, pl.ds(b * LANES, LANES)], pout_sem.at[len(outs) - 4])
-            out.start()
-            outs.append(out)
+    for c in lasts:
+        c.wait_recv()
     for c in firsts + seconds + thirds + fourths + fifths + lasts:
         c.wait_send()
     for k in range(2):
         when_each(sides[k][1], across[k].wait_send)
         when_each(corners[k][1], diagonal[k].wait_send)
-    for out in outs:
-        out.wait()
 
 
 def collect(acc, term):
@@ -515,26 +531,48 @@
     return pl.pallas_call(
         gather_kernel,
         in_specs=[pl.BlockSpec(memory_space=pl.ANY)] * 2,
-        out_specs=[pl.BlockSpec(memory_space=pl.ANY)] * 2,
-        out_shape=[jax.ShapeDtypeStruct((2, 256, 512), F32), jax.ShapeDtypeStruct((2, 256, 256), F32)],
+        out_specs=[pl.BlockSpec(memory_space=pltpu.VMEM)] * 2,
+        out_shape=[jax.ShapeDtypeStruct((2, 4, 2 * RIM, LANES), F32), jax.ShapeDtypeStruct((1024, LANES), F32)],
         scratch_shapes=[
-            vmem(2, 4, 2 * RIM, LANES), vmem(1024, LANES), vmem(1024, LANES),
+            vmem(1024, LANES),
             vmem(2, 4, RIM, LANES), vmem(2, 4, RIM, LANES), vmem(2, 2, RIM, LANES), vmem(2, 2, 2 * RIM, LANES),
             vmem(2, 2, RIM, LANES), vmem(2, 2, 2 * RIM, LANES),
             vmem(4, 128, LANES), vmem(3, 128, LANES), vmem(15, 8, LANES),
             dma((4,)), dma((8,)), dma((8,)), dma((4,)), dma((4,)), dma((3,)), dma((3,)), dma((15,)), dma((15,)),
-            dma((15,)), dma((15,)), dma((3,)), dma((3,)), dma((4,)), dma((4,)), dma((4,)), dma((4,)),
+            dma((15,)), dma((15,)), dma((3,)), dma((3,)), dma((4,)), dma((4,)),
         ],
         compiler_params=pltpu.CompilerParams(collective_id=1, has_side_effects=True, vmem_limit_bytes=16 * 2**20),
         name="collect",
     )(acc, term.reshape(1024, LANES))
 
 
+def layout_kernel(own_ref, sum_ref, obj_ref, probe_ref, sem):
+    copies = [pltpu.make_async_copy(own_ref.at[:, b], obj_ref.at[:, :, pl.ds(b * LANES, LANES)], sem.at[b]) for b in range(4)]
+    copies += [pltpu.make_async_copy(sum_ref.at[i // 2, i % 2], probe_ref.at[i // 2, :, pl.ds((i % 2) * LANES, LANES)], sem.at[4 + i])
+               for i in range(4)]
+    for copy in copies:
+        copy.start()
+    for copy in copies:
+        copy.wait()
+
+
+def laid_out(own, probe_sum):
+    return pl.pallas_call(
+        layout_kernel,
+        in_specs=[pl.BlockSpec(memory_space=pltpu.VMEM)] * 2,
+        out_specs=[pl.BlockSpec(memory_space=pl.ANY)] * 2,
+        out_shape=[jax.ShapeDtypeStruct((2, 2 * RIM, 4 * LANES), F32), jax.ShapeDtypeStruct((2, 2 * RIM, 2 * LANES), F32)],
+        scratch_shapes=[pltpu.SemaphoreType.DMA((8,))],
+        compiler_params=pltpu.CompilerParams(vmem_limit_bytes=4 * 2**20),
+        name="layout",
+    )(own, probe_sum.reshape(2, 2, 2 * RIM, LANES))
+
+
 def on_device(object_field, probe_field, measured, offsets):
     fixed = [pltpu.with_memory_space_constraint(a, pltpu.HBM) for a in (object_field, measured, probe_field)]
     ext, ordered, probe = exchange(*fixed)
-    acc, term = compute(offsets.T, ext, probe, ordered, jnp.asarray(dft_tables(256)))
-    return collect(acc, term)
+    acc, term = compute(offsets.T, ext, probe, ordered, jnp.asarray(dft_tables(256)), jnp.asarray(row_tables(256)))
+    return tuple(laid_out(*collect(acc, term)))
 
 
 def solution(mesh):

time: 71.1 us -> 69.6 us (0.979)
  local copies, waits for them, and re-layouts: 1.78 us -> 0.02 us
    unnamed x6, local copies, waits for them, and re-layouts: 1.78 us -> 0.02 us
    pallas_call x0 -> x1, Pallas kernels: none -> 1.2 us  [laid_out(): pl.pallas_call(layout_kernel, in_specs=[pl.BlockSpec(memory_space=pltpu.V...]
    pallas_call x1, Pallas kernels: 20.9 us -> 20.1 us  [compute(): pl.pallas_call(functools.partial(compute_kernel, per_step, chunk), in_spe...]
where the time goes in v4:
time: 69.6 us; the launch traced here: 69.1 us
  Pallas kernels  68.4 us (98%)
  between operations  0.7 us (1%)
    pallas_call x1, Pallas kernels, collect(): pl.pallas_call(gather_kernel, in_specs=[pl.BlockSpec(memory_space=pl.ANY)...  32 us
    pallas_call x1, Pallas kernels, compute(): pl.pallas_call(functools.partial(compute_kernel, per_step, chunk), in_spe...  20.1 us
    pallas_call x1, Pallas kernels, exchange(): pl.pallas_call(halo_kernel, in_specs=[pl.BlockSpec(memory_space=pltpu.HBM...  15 us

profile of v4, /device:TPU:1, one launch (start us, length us, event | category | flops | bytes accessed | tf_op | source)
XLA Modules:
  0.0 69.1 jit_solution(12019935817979242954)
XLA Ops:
  0.6 0.0 copy-start
  0.6 0.0 copy-start.1
  0.7 0.0 copy-start.2
  0.7 15.0 %halo.1 = (f32[2,6,512,128]{3,2,1,0:T(8,128)S(1)}, f32[16,256,256]{2,1,0:T(8,128)S(1)}, f32[2,2,256,128]{3,2,1,0:T(8,128)S(1)}) custom-call(f32[2,256,512]{2,1,0:T(8,128)} %obj_ref.1, f32[16,256,256]{2,1,0:T(8,128)} %meas_ref.1, f32[2,256,256]{2,1,0:T(8,128)} %prb_ref.1), custom_call_target="tpu_custom_call" | custom-call | tf_op jit(solution)/shard_map/halo/pallas_call | solution.py:365
  15.7 0.0 copy-done
  15.7 0.0 copy-done.1
  15.7 0.0 copy-done.2
  15.7 20.1 %updates.1 = (f32[2,6,512,128]{3,2,1,0:T(8,128)S(1)}, f32[2,2,256,128]{3,2,1,0:T(8,128)S(1)}) custom-call(s32[2,16]{1,0:T(2,128)S(1)} %bitcast.5, f32[2,6,512,128]{3,2,1,0:T(8,128)S(1)} %get-tuple-element.9.ext_ref, f32[2,2,256,128]{3,2,1,0:T(8,128)S(1)} %get-tuple-element.10.probe_ref, f32[16,256,256]{2,1,0:T(8,128)S(1)} %get-tuple-element.11.meas_ref, ...), custom_call_target="tpu_custom_call" | custom-call | tf_op jit(solution)/shard_map/updates/pallas_call | solution.py:205
  35.9 32.0 %collect.1 = (f32[2,4,256,128]{3,2,1,0:T(8,128)S(1)}, f32[1024,128]{1,0:T(8,128)S(1)}) custom-call(f32[2,6,512,128]{3,2,1,0:T(8,128)S(1)} %get-tuple-element.12.acc_ref, f32[1024,128]{1,0:T(8,128)S(1)} %bitcast.3), custom_call_target="tpu_custom_call" | custom-call | tf_op jit(solution)/shard_map/collect/pallas_call | solution.py:531
  67.9 1.2 %layout.1 = (f32[2,256,512]{2,1,0:T(8,128)}, f32[2,256,256]{2,1,0:T(8,128)}) custom-call(f32[2,4,256,128]{3,2,1,0:T(8,128)S(1)} %get-tuple-element.14.own_ref, f32[2,2,256,128]{3,2,1,0:T(8,128)S(1)} %bitcast.4), custom_call_target="tpu_custom_call" | custom-call | tf_op jit(solution)/shard_map/layout/pallas_call | solution.py:560
Async XLA Ops:
  0.6 15.1 %copy-start = (bf16[2,4,256,256]{3,2,1,0:T(8,128)(2,1)S(1)}, bf16[2,4,256,256]{3,2,1,0:T(8,128)(2,1)}, u32[]{:S(2)}) copy-start(bf16[2,4,256,256]{3,2,1,0:T(8,128)(2,1)} %constant.5.clone.rtab_ref) | copy-start | bytes 3145732
  0.6 15.1 %copy-start.1 = (bf16[4,2,256,256]{3,2,1,0:T(8,128)(2,1)S(1)}, bf16[4,2,256,256]{3,2,1,0:T(8,128)(2,1)}, u32[]{:S(2)}) copy-start(bf16[4,2,256,256]{3,2,1,0:T(8,128)(2,1)} %constant.4.clone.tab_ref) | copy-start | bytes 3145732
  0.7 15.1 %copy-start.2 = (s32[16,2]{0,1:T(2,128)S(1)}, s32[16,2]{0,1:T(2,128)}, u32[]{:S(2)}) copy-start(s32[16,2]{0,1:T(2,128)} %param.9) | copy-start | bytes 388

commit v5 on v4

--- a/solution.py
+++ b/solution.py
@@ -272,10 +272,9 @@
                 for b in range(2)]
     sides = [neighbour(0, -1), neighbour(0, 1)]
     outer, outer_in = neighbour(-inner, 0)
-    corners = [neighbour(-inner, -1), neighbour(-inner, 1)]
     for load in loads:
         load.start()
-    greet(sides + corners + [(outer, outer_in), (partner, p >= 0)])
+    greet(sides + [(outer, outer_in), (partner, p >= 0)])
     inner_row = pl.multiple_of((1 - core) * RIM, RIM)
     outer_row = pl.multiple_of(core * RIM, RIM)
     inner_halo = pl.multiple_of((1 - core) * 3 * RIM, RIM)
@@ -291,13 +290,18 @@
         pairs.append((copy, there, source_there, fill))
         when_each(there, copy.start)
 
-    add(0, 2 * RIM, 0, 5, RIM, sides[0][0], sides[0][1], sides[1][1], RIM)
-    add(0, 2 * RIM, 3, 0, RIM, sides[1][0], sides[1][1], sides[0][1], RIM)
+    inner_own = pl.multiple_of((2 - core) * RIM, RIM)
+    outer_own = pl.multiple_of((1 + core) * RIM, RIM)
     there_row = pl.multiple_of((1 - core) * 3 * RIM, RIM)
+
+    def add_sides(row, own_row):
+        add(row, RIM, 0, 5, own_row, sides[0][0], sides[0][1], sides[1][1], own_row)
+        add(row, RIM, 3, 0, own_row, sides[1][0], sides[1][1], sides[0][1], own_row)
+
+    add_sides(outer_row, outer_own)
     for b in range(4):
         add(outer_row, RIM, b, b + 1, there_row, outer, outer_in, outer_in, outer_halo)
-    add(outer_row, RIM, 0, 5, there_row, corners[0][0], corners[0][1], corners[1][1], outer_halo)
-    add(outer_row, RIM, 3, 0, there_row, corners[1][0], corners[1][1], corners[0][1], outer_halo)
+    add_sides(inner_row, inner_own)
     partner_halo = pl.multiple_of(core * 3 * RIM, RIM)
     inside = [remote(obj_ref.at[:, pl.ds(inner_row, RIM), pl.ds(b * LANES, LANES)],
                      ext_ref.at[:, b + 1, pl.ds(partner_halo, RIM), :], relay_send.at[b], relay_recv.at[b], partner)
@@ -312,18 +316,28 @@
     perm_rows, perm_cols = order_table(True, size), order_table(False, size)
     stores = []
 
-    def relay():
-        made = []
-        inner_own = pl.multiple_of((2 - core) * RIM, RIM)
+    def side_landed(k):
+        copy, _, source_there, fill = pairs[k]
+        when_each(source_there, copy.wait_recv)
+        when_each(jnp.logical_not(source_there), fill.wait)
+
+    edge, edge_fill = [], []
+
+    def relay_edge():
         for k, block in enumerate((5, 0)):
-            copy, there, source_there, fill = pairs[k]
-            when_each(source_there, copy.wait_recv)
-            when_each(jnp.logical_not(source_there), fill.wait)
-            here = ext_ref.at[:, block, pl.ds(inner_own, RIM), :]
-            there_ref = ext_ref.at[:, block, pl.ds(partner_halo, RIM), :]
-            made.append(remote(here, there_ref, relay_send.at[4 + k], relay_recv.at[4 + k], partner))
-            made[-1].start()
-        return made
+            side_landed(k)
+            edge.append(remote(ext_ref.at[:, block, pl.ds(outer_own, RIM), :], ext_ref.at[:, block, pl.ds(there_row, RIM), :],
+                               relay_send.at[6 + k], relay_recv.at[6 + k], outer))
+            edge_fill.append(pltpu.make_async_copy(zeros, ext_ref.at[:, block, pl.ds(outer_halo, RIM), :], fill_sem.at[8 + k]))
+            when_each(outer_in, edge[k].start)
+            when_each(jnp.logical_not(outer_in), edge_fill[k].start)
+
+    def relay_inner():
+        for k, block in enumerate((5, 0)):
+            side_landed(6 + k)
+            inside.append(remote(ext_ref.at[:, block, pl.ds(inner_own, RIM), :], ext_ref.at[:, block, pl.ds(partner_halo, RIM), :],
+                                 relay_send.at[4 + k], relay_recv.at[4 + k], partner))
+            inside[-1].start()
 
     for g in range(in_sem.shape[0]):
         loads[g].wait()
@@ -346,16 +360,20 @@
         store = pltpu.make_async_copy(ordered.at[pl.ds(g * group, group)], out_ref.at[pl.ds(g * group, group)], out_sem.at[g])
         store.start()
         stores.append(store)
-    inside += relay()
+        if g == in_sem.shape[0] - 2:
+            relay_edge()
+    relay_inner()
     for copy in stores + locals_:
         copy.wait()
     for index, (copy, there, source_there, fill) in enumerate(pairs):
         when_each(there, copy.wait_send)
-        if index >= 2:
-            when_each(source_there, copy.wait_recv)
-            when_each(jnp.logical_not(source_there), fill.wait)
+        if 2 <= index < 6:
+            side_landed(index)
     for copy in inside:
         copy.wait()
+    for k in range(2):
+        when_each(outer_in, edge[k].wait)
+        when_each(jnp.logical_not(outer_in), edge_fill[k].wait)
 
 
 def exchange(object_field, measured, probe_field):
@@ -369,11 +387,11 @@
         out_shape=[jax.ShapeDtypeStruct((2, 6, 4 * RIM, LANES), F32), jax.ShapeDtypeStruct(measured.shape, F32),
                    jax.ShapeDtypeStruct((2, 2, 2 * RIM, LANES), F32)],
         scratch_shapes=[
-            pltpu.VMEM((2, 2 * RIM, LANES), F32),
+            pltpu.VMEM((2, RIM, LANES), F32),
             pltpu.VMEM(measured.shape, F32),
             pltpu.VMEM(measured.shape, F32),
-            dma((8,)), dma((8,)), dma((8,)),
-            dma((4,)), dma((groups,)), dma((groups,)), dma((6,)), dma((6,)), dma((2,)),
+            dma((8,)), dma((8,)), dma((10,)),
+            dma((4,)), dma((groups,)), dma((groups,)), dma((8,)), dma((8,)), dma((2,)),
         ],
         compiler_params=pltpu.CompilerParams(collective_id=0, has_side_effects=True, vmem_limit_bytes=16 * 2**20),
         name="halo",

time: 69.6 us -> 68.3 us (0.981)
  Pallas kernels: 68.4 us -> 67.3 us
    pallas_call x1, Pallas kernels: 32 us -> 30.3 us  [collect(): pl.pallas_call(gather_kernel, in_specs=[pl.BlockSpec(memory_space=pl.ANY)...]
where the time goes in v5:
time: 68.3 us; the launch traced here: 68 us
  Pallas kernels  67.3 us (99%)
  between operations  0.7 us (1%)
    pallas_call x1, Pallas kernels, collect(): pl.pallas_call(gather_kernel, in_specs=[pl.BlockSpec(memory_space=pl.ANY)...  30.3 us
    pallas_call x1, Pallas kernels, compute(): pl.pallas_call(functools.partial(compute_kernel, per_step, chunk), in_spe...  20.1 us
    pallas_call x1, Pallas kernels, exchange(): pl.pallas_call(halo_kernel, in_specs=[pl.BlockSpec(memory_space=pltpu.HBM...  15.7 us

profile of v5, /device:TPU:1, one launch (start us, length us, event | category | flops | bytes accessed | tf_op | source)
XLA Modules:
  0.0 68.0 jit_solution(8711005985295953597)
XLA Ops:
  0.6 0.0 copy-start
  0.6 0.0 copy-start.1
  0.7 0.0 copy-start.2
  0.7 15.7 %halo.1 = (f32[2,6,512,128]{3,2,1,0:T(8,128)S(1)}, f32[16,256,256]{2,1,0:T(8,128)S(1)}, f32[2,2,256,128]{3,2,1,0:T(8,128)S(1)}) custom-call(f32[2,256,512]{2,1,0:T(8,128)} %obj_ref.1, f32[16,256,256]{2,1,0:T(8,128)} %meas_ref.1, f32[2,256,256]{2,1,0:T(8,128)} %prb_ref.1), custom_call_target="tpu_custom_call" | custom-call | tf_op jit(solution)/shard_map/halo/pallas_call | solution.py:383
  16.4 0.0 copy-done
  16.4 0.0 copy-done.1
  16.4 0.0 copy-done.2
  16.4 20.1 %updates.1 = (f32[2,6,512,128]{3,2,1,0:T(8,128)S(1)}, f32[2,2,256,128]{3,2,1,0:T(8,128)S(1)}) custom-call(s32[2,16]{1,0:T(2,128)S(1)} %bitcast.5, f32[2,6,512,128]{3,2,1,0:T(8,128)S(1)} %get-tuple-element.9.ext_ref, f32[2,2,256,128]{3,2,1,0:T(8,128)S(1)} %get-tuple-element.10.probe_ref, f32[16,256,256]{2,1,0:T(8,128)S(1)} %get-tuple-element.11.meas_ref, ...), custom_call_target="tpu_custom_call" | custom-call | tf_op jit(solution)/shard_map/updates/pallas_call | solution.py:205
  36.5 30.3 %collect.1 = (f32[2,4,256,128]{3,2,1,0:T(8,128)S(1)}, f32[1024,128]{1,0:T(8,128)S(1)}) custom-call(f32[2,6,512,128]{3,2,1,0:T(8,128)S(1)} %get-tuple-element.12.acc_ref, f32[1024,128]{1,0:T(8,128)S(1)} %bitcast.3), custom_call_target="tpu_custom_call" | custom-call | tf_op jit(solution)/shard_map/collect/pallas_call | solution.py:549
  66.8 1.2 %layout.1 = (f32[2,256,512]{2,1,0:T(8,128)}, f32[2,256,256]{2,1,0:T(8,128)}) custom-call(f32[2,4,256,128]{3,2,1,0:T(8,128)S(1)} %get-tuple-element.14.own_ref, f32[2,2,256,128]{3,2,1,0:T(8,128)S(1)} %bitcast.4), custom_call_target="tpu_custom_call" | custom-call | tf_op jit(solution)/shard_map/layout/pallas_call | solution.py:578
Async XLA Ops:
  0.6 15.7 %copy-start = (bf16[2,4,256,256]{3,2,1,0:T(8,128)(2,1)S(1)}, bf16[2,4,256,256]{3,2,1,0:T(8,128)(2,1)}, u32[]{:S(2)}) copy-start(bf16[2,4,256,256]{3,2,1,0:T(8,128)(2,1)} %constant.5.clone.rtab_ref) | copy-start | bytes 3145732
  0.6 15.7 %copy-start.1 = (bf16[4,2,256,256]{3,2,1,0:T(8,128)(2,1)S(1)}, bf16[4,2,256,256]{3,2,1,0:T(8,128)(2,1)}, u32[]{:S(2)}) copy-start(bf16[4,2,256,256]{3,2,1,0:T(8,128)(2,1)} %constant.4.clone.tab_ref) | copy-start | bytes 3145732
  0.7 15.7 %copy-start.2 = (s32[16,2]{0,1:T(2,128)S(1)}, s32[16,2]{0,1:T(2,128)}, u32[]{:S(2)}) copy-start(s32[16,2]{0,1:T(2,128)} %param.9) | copy-start | bytes 388

commit v6 on v5

--- a/solution.py
+++ b/solution.py
@@ -97,6 +97,8 @@
         e0i = p0r * x0i + p0i * x0r
         e1r = p1r * x1r - p1i * x1i
         e1i = p1r * x1i + p1i * x1r
+        if start + chunk == size // 2:
+            yield
         sums.append(cat([split(e0r + e1r), split(e0i + e1i)], 1))
         diffs.append(cat([split(e0r - e1r), split(e0i - e1i)], 1))
     a, b = cat(sums, 0), cat(diffs, 0)
@@ -176,12 +178,12 @@
             r1 = pltpu.roll(t1, back_shift, 1)
             term_ref[plane, 0, rows, :] += jnp.where(keep, r0, r1)
             term_ref[plane, 1, rows, :] += jnp.where(keep, r1, r0)
-
-
-def compute_kernel(per_step, chunk, off_ref, ext_ref, probe_ref, meas_ref, tab_ref, rtab_ref, acc_ref, term_ref, rolled):
-    acc_ref[...] = jnp.zeros_like(acc_ref)
-    term_ref[...] = jnp.zeros_like(term_ref)
-    stages = 9
+        if start + chunk == size // 2:
+            yield
+
+
+def compute_kernel(per_step, chunk, off_ref, ext_ref, probe_ref, meas_ref, tab_ref, rtab_ref, zero_acc, zero_term, acc_ref, term_ref, rolled):
+    stages = 11
 
     def step(index, carry):
         live = []
@@ -200,17 +202,18 @@
     lax.fori_loop(0, meas_ref.shape[0] // per_step, step, 0)
 
 
-def compute(offsets, ext, probe, meas, tables, rows, per_step=4, chunk=32):
+def compute(offsets, ext, probe, meas, tables, rows, acc, term, per_step=4, chunk=32):
     vmem = pl.BlockSpec(memory_space=pltpu.VMEM)
     return pl.pallas_call(
         functools.partial(compute_kernel, per_step, chunk),
-        in_specs=[pl.BlockSpec(memory_space=pltpu.SMEM)] + [vmem] * 5,
+        in_specs=[pl.BlockSpec(memory_space=pltpu.SMEM)] + [vmem] * 7,
         out_specs=[vmem] * 2,
         out_shape=[jax.ShapeDtypeStruct(ext.shape, F32), jax.ShapeDtypeStruct(probe.shape, F32)],
         scratch_shapes=[pltpu.VMEM((per_step, 2, 2, 256, 128), F32)],
         compiler_params=pltpu.CompilerParams(vmem_limit_bytes=32 * 2**20),
+        input_output_aliases={6: 0, 7: 1},
         name="updates",
-    )(offsets, ext, probe, meas, tables, rows)
+    )(offsets, ext, probe, meas, tables, rows, acc, term)
 
 
 POS, TILE = "pos", "tile"
@@ -258,7 +261,7 @@
     return jnp.where(src == wanted, 1.0, 0.0).astype(BF16)
 
 
-def halo_kernel(obj_ref, meas_ref, prb_ref, ext_ref, out_ref, probe_ref, zeros, loaded, ordered, send_sem, recv_sem,
+def halo_kernel(obj_ref, meas_ref, prb_ref, ext_ref, out_ref, probe_ref, acc_ref, term_ref, zeros, loaded, ordered, send_sem, recv_sem,
                 fill_sem, own_sem, in_sem, out_sem, relay_send, relay_recv, probe_sem):
     group = loaded.shape[0] // in_sem.shape[0]
     size = loaded.shape[1]
@@ -311,6 +314,8 @@
     for copy in locals_:
         copy.start()
     zeros[...] = jnp.zeros_like(zeros)
+    acc_ref[...] = jnp.zeros_like(acc_ref)
+    term_ref[...] = jnp.zeros_like(term_ref)
     for copy, there, source_there, fill in pairs:
         when_each(jnp.logical_not(source_there), fill.start)
     perm_rows, perm_cols = order_table(True, size), order_table(False, size)
@@ -383,8 +388,9 @@
     return pl.pallas_call(
         halo_kernel,
         in_specs=[pl.BlockSpec(memory_space=pltpu.HBM)] * 3,
-        out_specs=[anywhere] * 3,
+        out_specs=[anywhere] * 3 + [pl.BlockSpec(memory_space=pltpu.VMEM)] * 2,
         out_shape=[jax.ShapeDtypeStruct((2, 6, 4 * RIM, LANES), F32), jax.ShapeDtypeStruct(measured.shape, F32),
+                   jax.ShapeDtypeStruct((2, 2, 2 * RIM, LANES), F32), jax.ShapeDtypeStruct((2, 6, 4 * RIM, LANES), F32),
                    jax.ShapeDtypeStruct((2, 2, 2 * RIM, LANES), F32)],
         scratch_shapes=[
             pltpu.VMEM((2, RIM, LANES), F32),
@@ -588,8 +594,8 @@
 
 def on_device(object_field, probe_field, measured, offsets):
     fixed = [pltpu.with_memory_space_constraint(a, pltpu.HBM) for a in (object_field, measured, probe_field)]
-    ext, ordered, probe = exchange(*fixed)
-    acc, term = compute(offsets.T, ext, probe, ordered, jnp.asarray(dft_tables(256)), jnp.asarray(row_tables(256)))
+    ext, ordered, probe, acc, term = exchange(*fixed)
+    acc, term = compute(offsets.T, ext, probe, ordered, jnp.asarray(dft_tables(256)), jnp.asarray(row_tables(256)), acc, term)
     return tuple(laid_out(*collect(acc, term)))
 
 

time: 68.3 us -> 67.8 us (level)
  no operation moved by 1% of the time
where the time goes in v6:
time: 67.8 us; the launch traced here: 67.5 us
  Pallas kernels  66.8 us (99%)
  between operations  0.7 us (1%)
    pallas_call x1, Pallas kernels, collect(): pl.pallas_call(gather_kernel, in_specs=[pl.BlockSpec(memory_space=pl.ANY)...  30.4 us
    pallas_call x1, Pallas kernels, compute(): pl.pallas_call(functools.partial(compute_kernel, per_step, chunk), in_spe...  19.5 us
    pallas_call x1, Pallas kernels, exchange(): pl.pallas_call(halo_kernel, in_specs=[pl.BlockSpec(memory_space=pltpu.HBM...  15.7 us

profile of v6, /device:TPU:1, one launch (start us, length us, event | category | flops | bytes accessed | tf_op | source)
XLA Modules:
  0.0 67.5 jit_solution(18171407381610350482)
XLA Ops:
  0.6 0.0 copy-start
  0.6 0.0 copy-start.1
  0.7 0.0 copy-start.2
  0.7 15.7 %halo.1 = (f32[2,6,512,128]{3,2,1,0:T(8,128)S(1)}, f32[16,256,256]{2,1,0:T(8,128)S(1)}, f32[2,2,256,128]{3,2,1,0:T(8,128)S(1)}, f32[2,6,512,128]{3,2,1,0:T(8,128)S(1)}, f32[2,2,256,128]{3,2,1,0:T(8,128)S(1)}) custom-call(f32[2,256,512]{2,1,0:T(8,128)} %obj_ref.1, f32[16,256,256]{2,1,0:T(8,128)} %meas_ref.1, f32[2,256,256]{2,1,0:T(8,128)} %prb_ref.1), custom_call_target="tpu_custom_call" | custom-call | tf_op jit(solution)/shard_map/halo/pallas_call | solution.py:388
  16.4 0.0 copy-done
  16.4 0.0 copy-done.1
  16.4 0.0 copy-done.2
  16.4 19.5 %updates.1 = (f32[2,6,512,128]{3,2,1,0:T(8,128)S(1)}, f32[2,2,256,128]{3,2,1,0:T(8,128)S(1)}) custom-call(s32[2,16]{1,0:T(2,128)S(1)} %bitcast.5, f32[2,6,512,128]{3,2,1,0:T(8,128)S(1)} %get-tuple-element.11.ext_ref, f32[2,2,256,128]{3,2,1,0:T(8,128)S(1)} %get-tuple-element.12.probe_ref, ...), custom_call_target="tpu_custom_call", output_to_operand_aliasing={{0}: (6, {}), {1}: (7, {})} | custom-call | tf_op jit(solution)/shard_map/updates/pallas_call | solution.py:207
  36.0 30.4 %collect.1 = (f32[2,4,256,128]{3,2,1,0:T(8,128)S(1)}, f32[1024,128]{1,0:T(8,128)S(1)}) custom-call(f32[2,6,512,128]{3,2,1,0:T(8,128)S(1)} %get-tuple-element.16.acc_ref, f32[1024,128]{1,0:T(8,128)S(1)} %bitcast.3), custom_call_target="tpu_custom_call" | custom-call | tf_op jit(solution)/shard_map/collect/pallas_call | solution.py:555
  66.3 1.2 %layout.1 = (f32[2,256,512]{2,1,0:T(8,128)}, f32[2,256,256]{2,1,0:T(8,128)}) custom-call(f32[2,4,256,128]{3,2,1,0:T(8,128)S(1)} %get-tuple-element.18.own_ref, f32[2,2,256,128]{3,2,1,0:T(8,128)S(1)} %bitcast.4), custom_call_target="tpu_custom_call" | custom-call | tf_op jit(solution)/shard_map/layout/pallas_call | solution.py:584
Async XLA Ops:
  0.6 15.8 %copy-start = (bf16[2,4,256,256]{3,2,1,0:T(8,128)(2,1)S(1)}, bf16[2,4,256,256]{3,2,1,0:T(8,128)(2,1)}, u32[]{:S(2)}) copy-start(bf16[2,4,256,256]{3,2,1,0:T(8,128)(2,1)} %constant.5.clone.rtab_ref) | copy-start | bytes 3145732
  0.6 15.7 %copy-start.1 = (bf16[4,2,256,256]{3,2,1,0:T(8,128)(2,1)S(1)}, bf16[4,2,256,256]{3,2,1,0:T(8,128)(2,1)}, u32[]{:S(2)}) copy-start(bf16[4,2,256,256]{3,2,1,0:T(8,128)(2,1)} %constant.4.clone.tab_ref) | copy-start | bytes 3145732
  0.7 15.7 %copy-start.2 = (s32[16,2]{0,1:T(2,128)S(1)}, s32[16,2]{0,1:T(2,128)}, u32[]{:S(2)}) copy-start(s32[16,2]{0,1:T(2,128)} %param.9) | copy-start | bytes 388
